TPU v7x, 32 devices: a whole 2x2x4 slice. The times are simulated.
32 devices in a mesh: blk: 4 (over y, x), sub: 2 (over core), feat: 4 (over z).
Axes of the slice: x: 2, y: 2, z: 4, core: 2. Of those that a mesh axis runs over, the one named last changes fastest.
Arguments:
- sources: bfloat16 [65536, 1024], P(('blk', 'sub'), 'feat'), may hold values from -6 to 6
- adjacency: bfloat16 [8, 8, 64, 128, 128], P(('blk', 'sub')), may hold values from -0.15625 to 0.15625
- target_block: int32 [8, 8, 64], P(('blk', 'sub')), may hold values from 0 to 7
- source_block: int32 [8, 8, 64], P(('blk', 'sub')), may hold values from 0 to 63
- slot_counts: int32 [8, 8], P(('blk', 'sub')), may hold values from 1 to 64, as said below
- weight: bfloat16 [1024, 1024], P(None, 'feat'), may hold values from -0.1875 to 0.1875
Outputs:
- activated: bfloat16 [8192, 1024], P(('blk', 'sub'), 'feat')
Inputs may be any that keep to these rules, and one draw needn't show every extreme that they name: Every stripe and piece uses its first slot_counts slots; in every draw some stripe and piece uses all 64.
All inputs are finite; a program needn't handle non-finite values.
Results may differ from a plain program's by a relative error of at most 0.0049.
Values may be sent and summed in bfloat16 or wider, within the bound.
No kernel may reach another device: no remote copies, remote signals or barrier semaphores. Data moves between devices by JAX's collectives and lax.ppermute only.
A program may use at most 256 MiB of HBM per device.

v0:
```python
import jax
import jax.numpy as jnp
from jax import lax
from jax.sharding import PartitionSpec as P

BLOCK = 128
TGT_DEV = 1024


def local_products(adj_group, rows_group, cols_group, counts_group, blocks):
    slot_total = adj_group.shape[1]
    block_total = blocks.shape[0]
    target_total = TGT_DEV // BLOCK
    feat_width = blocks.shape[2]

    def one_piece(adj_piece, rows_piece, cols_piece, count_piece):
        source_hot = (
            cols_piece[:, None] == jnp.arange(block_total, dtype=jnp.int32)[None, :]
        ).astype(jnp.bfloat16)
        selected = jnp.einsum(
            "sk,kif->sif", source_hot, blocks, preferred_element_type=jnp.float32
        ).astype(jnp.bfloat16)
        product = jnp.einsum(
            "sij,sjf->sif", adj_piece, selected, preferred_element_type=jnp.float32
        )
        live_slots = jnp.arange(slot_total, dtype=jnp.int32) < count_piece
        target_hot = (
            (jnp.arange(target_total, dtype=jnp.int32)[:, None] == rows_piece[None, :])
            & live_slots[None, :]
        ).astype(jnp.float32)
        summed = jnp.einsum("ts,sif->tif", target_hot, product, precision=lax.Precision.HIGHEST)
        return summed.reshape(TGT_DEV, feat_width)

    return jax.vmap(one_piece)(adj_group, rows_group, cols_group, counts_group)


def body(sources, adjacency, target_block, source_block, slot_counts, weight):
    feat_width = sources.shape[1]
    blocks = sources.reshape(sources.shape[0] // BLOCK, BLOCK, feat_width)
    adj_local = adjacency[0]
    target_local = target_block[0]
    source_local = source_block[0]
    count_local = slot_counts[0]
    piece_terms = local_products(adj_local, target_local, source_local, count_local, blocks)
    summed = lax.psum_scatter(
        piece_terms.reshape(TGT_DEV * lax.axis_size(("blk", "sub")), feat_width),
        ("blk", "sub"),
        scatter_dimension=0,
        tiled=True,
    )
    hidden = summed.astype(jnp.bfloat16)
    projected = jnp.dot(
        lax.all_gather(hidden, "feat", axis=1, tiled=True),
        weight,
        preferred_element_type=jnp.float32,
    )
    return jax.nn.relu(projected).astype(jnp.bfloat16)


def solution(mesh):
    return jax.shard_map(
        body,
        mesh=mesh,
        in_specs=(
            P(("blk", "sub"), "feat"),
            P(("blk", "sub"), None, None, None, None),
            P(("blk", "sub"), None, None),
            P(("blk", "sub"), None, None),
            P(("blk", "sub"), None),
            P(None, "feat"),
        ),
        out_specs=P(("blk", "sub"), "feat"),
        check_vma=False,
    )
```

profile of v0, /device:TPU:0, one launch (start us, length us, event | category | flops | bytes accessed | tf_op | source)
XLA Modules:
  0.0 319.7 jit_solution(10508421565872982486)
XLA Ops:
  6.5 0.0 copy-start
  6.5 0.0 reduce-scatter.2.cloned.1.call-start
  6.5 18.8 %fusion.4 = bf16[8,64,128,256]{3,1,2,0:T(8,128)(2,1)} fusion(bf16[64,128,256,1]{2,1,0,3:T(8,128)(2,1)} %bitcast.26, s32[8,64]{1,0:T(8,128)} %bitcast.27), kind=kOutput, calls=%fused_computation.5 | convolution fusion | flops 2147516416 | bytes 37750784 | tf_op jit(solution)/shard_map/vmap(sk,kif->sif)/dot_general | solution.py:20
  25.3 55.4 %fusion.2 = f32[8,64,256,128]{3,2,1,0:T(8,128)} fusion(bf16[8,64,128,256]{3,1,2,0:T(8,128)(2,1)} %fusion.4, bf16[1,8,64,128,128]{4,3,2,1,0:T(8,128)(2,1)} %param.7), kind=kOutput, calls=%fused_computation.3 | convolution fusion | flops 4294967296 | bytes 117440512 | tf_op jit(solution)/shard_map/vmap(sij,sjf->sif)/dot_general | solution.py:23
  80.7 0.0 copy-start.2
  80.7 0.0 copy-start.1
  80.7 66.9 %copy.11 = f32[8,64,256,128]{2,1,3,0:T(8,128)} copy(f32[8,64,256,128]{3,2,1,0:T(8,128)} %fusion.2) | data formatting | bytes 134217728 | tf_op jit(solution)/shard_map/vmap(sij,sjf->sif)/dot_general | solution.py:23
  147.6 0.0 copy-done.2
  147.6 0.1 iota_compare_fusion.2
  147.6 0.0 copy-done.1
  147.6 30.4 %fusion = f32[8,8,128,256]{3,1,2,0:T(8,128)} fusion(f32[8,64,256,128]{2,1,3,0:T(8,128)} %copy.11, s32[8,64]{1,0:T(8,128)S(1)} %bitcast.28, pred[8,64]{1,0:T(8,128)(4,1)S(1)} %iota_compare_fusion.2), kind=kOutput, calls=%fused_computation | convolution fusion | flops 1610620928 | bytes 75500032 | tf_op jit(solution)/shard_map/vmap(ts,sif->tif)/dot_general | solution.py:31
  178.1 9.1 %copy.7 = f32[8,8,128,256]{3,2,1,0:T(8,128)} copy(f32[8,8,128,256]{3,1,2,0:T(8,128)} %fusion) | data formatting | bytes 16777216 | tf_op jit(solution)/shard_map/vmap(ts,sif->tif)/dot_general | solution.py:31
  187.2 0.0 reduce-scatter.2.cloned.1.call-update
  187.2 0.0 all-gather.2.cloned.1.call-start
  187.2 74.1 %reduce-scatter.2.cloned.1.call-done = f32[1024,256]{1,0:T(8,128)} async-done(((f32[8192,256]{1,0:T(8,128)}), f32[1024,256]{1,0:T(8,128)}) %reduce-scatter.2.cloned.1.call-update) | async-done | bytes 1048592 | tf_op jit(solution)/shard_map/reduce_scatter | solution.py:45
  261.3 2.1 convert_element_type.12
  263.4 0.0 all-gather.2.cloned.1.call-update
  263.4 46.4 %all-gather.2.cloned.1.call-done = bf16[1024,1024]{1,0:T(8,128)(2,1)} async-done(((bf16[1024,256]{1,0:T(8,128)(2,1)}), bf16[1024,1024]{1,0:T(8,128)(2,1)}) %all-gather.2.cloned.1.call-update) | async-done | bytes 2097168 | tf_op jit(solution)/shard_map/all_gather | solution.py:53
  309.8 0.0 copy-done
  309.8 3.1 fusion.6
Async XLA Ops:
  6.5 303.3 %copy-start = (bf16[1024,256]{1,0:T(8,128)(2,1)S(1)}, bf16[1024,256]{1,0:T(8,128)(2,1)}, u32[]{:S(2)}) copy-start(bf16[1024,256]{1,0:T(8,128)(2,1)} %param.11) | copy-start | bytes 1572868
  6.5 254.8 %reduce-scatter.2.cloned.1.call-start = ((), (), s32[]{:S(2)}) async-start(), calls=%async_computation.1 | async-start | bytes 9437184 | tf_op jit(solution)/shard_map/reduce_scatter | solution.py:45
  80.7 66.9 %copy-start.2 = (s32[1,8]{1,0:T(1,128)S(1)}, s32[1,8]{1,0:T(1,128)}, u32[]{:S(2)}) copy-start(s32[1,8]{1,0:T(1,128)} %param.10) | copy-start | bytes 100
  80.7 66.9 %copy-start.1 = (s32[1,8,64]{2,1,0:T(8,128)S(1)}, s32[1,8,64]{2,1,0:T(8,128)}, u32[]{:S(2)}) copy-start(s32[1,8,64]{2,1,0:T(8,128)} %param.8) | copy-start | bytes 6148
  187.2 122.6 %all-gather.2.cloned.1.call-start = ((), (), s32[]{:S(2)}) async-start(), calls=%async_computation.2 | async-start | bytes 2621440 | tf_op jit(solution)/shard_map/all_gather | solution.py:53
Sparse Core Ops, SparseCore 0:
  187.3 73.9 reduce-scatter.1
  263.5 46.2 all-gather.1
where the time goes:
time: 321 us; the launch traced here: 320 us
  waiting for transfers between devices  120 us (37%)
  matrix products  108 us (34%)
  local copies, waits for them, and re-layouts  76 us (24%)
  between operations  13.4 us (4%)
    reduce_scatter x1, waiting for transfers between devices, body(): lax.psum_scatter(piece_terms.reshape(TGT_DEV * lax.axis_size(('blk', 'sub...  74.1 us
    dot_general x1, local copies, waits for them, and re-layouts, one_piece(): jnp.einsum('sij,sjf->sif', adj_piece, selected, preferred_element_type=jn...  66.9 us
    dot_general x1, matrix products, one_piece(): jnp.einsum('sij,sjf->sif', adj_piece, selected, preferred_element_type=jn...  55.4 us
    all_gather x1, waiting for transfers between devices, body(): lax.all_gather(hidden, 'feat', axis=1, tiled=True)  46.4 us
    dot_general x1, matrix products, one_piece(): jnp.einsum('ts,sif->tif', target_hot, product, precision=lax.Precision.HI...  30.4 us
    dot_general x1, matrix products, one_piece(): jnp.einsum('sk,kif->sif', source_hot, blocks, preferred_element_type=jnp....  18.8 us
    dot_general x1, local copies, waits for them, and re-layouts, one_piece(): jnp.einsum('ts,sif->tif', target_hot, product, precision=lax.Precision.HI...  9.11 us
  transfers between devices with their start and end apart: 2, of which 2 were waited for; matrix products, arithmetic and copies ran while one was open for 0% of the time, Pallas kernels for 0%

commit v1 on v0

v1 whole, which is shorter than its diff:
```python
import functools

import jax
import jax.numpy as jnp
from jax import lax
from jax.experimental import pallas as pl
from jax.experimental.pallas import tpu as pltpu
from jax.sharding import PartitionSpec as P

TGT_DEV = 1024
GROUP = 8
VMEM_BYTES = 48 * 2**20


def forward(index, step, size):
    if size & (size - 1) == 0:
        return index ^ step
    return (index + step) % size


def backward(index, step, size):
    if size & (size - 1) == 0:
        return index ^ step
    return (index + size - step) % size


def send(value, axis, step):
    size = lax.axis_size(axis)
    return lax.ppermute(value, axis, [(i, forward(i, step, size)) for i in range(size)])


def fetch(value, axis, step):
    size = lax.axis_size(axis)
    return lax.ppermute(value, axis, [(forward(i, step, size), i) for i in range(size)])


def products_kernel(target, source, count, ids, src_hbm, adj_hbm, out, src, adj, acc, src_sem, adj_sem):
    step = pl.program_id(0)
    pieces, slots, block, _ = adj.shape
    targets = acc.shape[0] - 1
    src_copy = pltpu.make_async_copy(src_hbm, src, src_sem)

    def tiles(piece, group):
        rows = pl.ds(group * GROUP, GROUP)
        return pltpu.make_async_copy(
            adj_hbm.at[ids[piece], rows], adj.at[piece, rows], adj_sem.at[piece, group]
        )

    def groups(piece):
        return (count[ids[piece]] + GROUP - 1) // GROUP

    @pl.when(step == 0)
    def _():
        src_copy.start()

        @pl.loop(0, pieces)
        def _(piece):
            @pl.loop(0, groups(piece))
            def _(group):
                tiles(piece, group).start()

        src_copy.wait()

    here = ids[step]
    acc[...] = jnp.zeros_like(acc)

    @pl.loop(0, groups(step))
    def _(group):
        tiles(step, group).wait()
        for lane in range(GROUP):
            slot = group * GROUP + lane
            row = jnp.where(slot < count[here], target[here, slot], targets)
            rows = pl.ds(pl.multiple_of(source[here, slot] * block, block), block)
            acc[row] += jnp.dot(adj[step, slot], src[rows, :], preferred_element_type=jnp.float32)

    for row in range(targets):
        out[0, row * block : (row + 1) * block, :] = acc[row].astype(out.dtype)


def products(sources, adjacency, target, source, count, ids):
    _, slots, block, _ = adjacency.shape
    pieces = ids.shape[0]
    feat = sources.shape[1]
    return pl.pallas_call(
        products_kernel,
        grid_spec=pltpu.PrefetchScalarGridSpec(
            num_scalar_prefetch=4,
            grid=(pieces,),
            in_specs=[pl.BlockSpec(memory_space=pl.ANY)] * 2,
            out_specs=pl.BlockSpec((1, TGT_DEV, feat), lambda step, *_: (step, 0, 0)),
            scratch_shapes=[
                pltpu.VMEM(sources.shape, sources.dtype),
                pltpu.VMEM((pieces, slots, block, block), adjacency.dtype),
                pltpu.VMEM((TGT_DEV // block + 1, block, feat), jnp.float32),
                pltpu.SemaphoreType.DMA,
                pltpu.SemaphoreType.DMA((pieces, slots // GROUP)),
            ],
        ),
        out_shape=jax.ShapeDtypeStruct((pieces, TGT_DEV, feat), jnp.bfloat16),
        compiler_params=pltpu.CompilerParams(vmem_limit_bytes=VMEM_BYTES),
        cost_estimate=pl.CostEstimate(
            flops=2 * pieces * slots * block * block * feat,
            bytes_accessed=2 * (sources.size + pieces * slots * block * block),
            transcendentals=0,
        ),
        name="products",
    )(target, source, count, ids, sources, adjacency)


def pair_sum_kernel(own, *refs):
    parts = own.shape[0]
    others, outs = refs[:-parts], refs[-parts:]
    for part in range(parts):
        total = own[part].astype(jnp.float32)
        for other in others:
            total += other[part].astype(jnp.float32)
        outs[part][...] = total.astype(outs[part].dtype)


def pair_sum(own, others):
    parts, rows, feat = own.shape
    tile = rows // 4
    return pl.pallas_call(
        pair_sum_kernel,
        grid=(rows // tile,),
        in_specs=[pl.BlockSpec((parts, tile, feat), lambda i: (0, i, 0))] * (1 + len(others)),
        out_specs=[pl.BlockSpec((tile, feat), lambda i: (i, 0))] * parts,
        out_shape=[
            jax.ShapeDtypeStruct((rows, feat), jnp.float32 if part == 0 else jnp.bfloat16)
            for part in range(parts)
        ],
        cost_estimate=pl.CostEstimate(
            flops=own.size * len(others), bytes_accessed=6 * own.size, transcendentals=0
        ),
        name="pair_sum",
    )(own, *others)


def deal_kernel(places, own, *refs):
    quarters = places.shape[0]
    others, outs = refs[:-quarters], refs[-quarters:]
    rows = outs[0].shape[0]
    for quarter in range(quarters):
        here = pl.ds(pl.multiple_of(places[quarter] * rows, rows), rows)
        total = own[here, :]
        for other in others:
            total += other[here, :].astype(jnp.float32)
        outs[quarter][...] = total.astype(jnp.bfloat16)


def deal(places, own, others):
    quarters = places.shape[0]
    rows, feat = own.shape
    vmem = pl.BlockSpec(memory_space=pltpu.VMEM)
    return pl.pallas_call(
        deal_kernel,
        in_specs=[pl.BlockSpec(memory_space=pltpu.SMEM)] + [vmem] * (1 + len(others)),
        out_specs=[vmem] * quarters,
        out_shape=[jax.ShapeDtypeStruct((rows // quarters, feat), jnp.bfloat16)] * quarters,
        cost_estimate=pl.CostEstimate(
            flops=own.size * len(others), bytes_accessed=10 * own.size, transcendentals=0
        ),
        name="deal",
    )(places, own, *others)


def layer_kernel(places, *refs):
    parts = places.shape[0]
    hidden, weights, outs = refs[:parts], refs[parts : 2 * parts], refs[2 * parts :]
    depth = hidden[0].shape[1]
    for part in range(parts):
        total = None
        for inner in range(parts):
            rows = pl.ds(pl.multiple_of(places[inner] * depth, depth), depth)
            term = jnp.dot(
                hidden[inner][...], weights[part][rows, :], preferred_element_type=jnp.float32
            )
            total = term if total is None else total + term
        outs[part][...] = jnp.maximum(total, 0.0).astype(outs[part].dtype)


def layer(places, hidden, weights):
    parts = len(hidden)
    rows = hidden[0].shape[0]
    depth, columns = weights[0].shape
    vmem = pl.BlockSpec(memory_space=pltpu.VMEM)
    return pl.pallas_call(
        layer_kernel,
        in_specs=[pl.BlockSpec(memory_space=pltpu.SMEM)] + [vmem] * (2 * parts),
        out_specs=[vmem] * parts,
        out_shape=[jax.ShapeDtypeStruct((rows, columns), jnp.bfloat16)] * parts,
        cost_estimate=pl.CostEstimate(
            flops=2 * rows * depth * columns * parts,
            bytes_accessed=2 * parts * depth * columns,
            transcendentals=0,
        ),
        name="layer",
    )(places, *hidden, *weights)


def gather_rows_kernel(places, *refs):
    out = refs[-1]
    for part, piece in enumerate(refs[:-1]):
        rows = piece.shape[0]
        out[pl.ds(pl.multiple_of(places[part] * rows, rows), rows), :] = piece[...]


def gather_rows(places, pieces):
    rows, columns = pieces[0].shape
    vmem = pl.BlockSpec(memory_space=pltpu.VMEM)
    return pl.pallas_call(
        gather_rows_kernel,
        in_specs=[pl.BlockSpec(memory_space=pltpu.SMEM)] + [vmem] * len(pieces),
        out_specs=vmem,
        out_shape=jax.ShapeDtypeStruct((rows * len(pieces), columns), pieces[0].dtype),
        name="gather_rows",
    )(places, *pieces)


def body(sources, adjacency, target_block, source_block, slot_counts, weight):
    blks, subs, feats = (lax.axis_size(axis) for axis in ("blk", "sub", "feat"))
    blk, sub, feat = (lax.axis_index(axis) for axis in ("blk", "sub", "feat"))

    def local(step):
        ids = jnp.stack(
            [forward(blk, part, blks) * subs + forward(sub, step, subs) for part in range(blks)]
        ).astype(jnp.int32)
        return products(
            sources, adjacency[0], target_block[0], source_block[0], slot_counts[0], ids
        )

    weights = [weight] + [fetch(weight, "feat", step) for step in range(1, feats)]
    arrived = [send(local(step), "sub", step) for step in range(1, subs)]
    chip = pair_sum(local(0), arrived)
    others = [send(chip[step], "blk", step) for step in range(1, blks)]
    ahead = jnp.stack([forward(feat, step, feats) for step in range(feats)]).astype(jnp.int32)
    behind = jnp.stack([backward(feat, step, feats) for step in range(feats)]).astype(jnp.int32)
    dealt = deal(ahead, chip[0], others)
    hidden = [dealt[0]] + [send(dealt[step], "feat", step) for step in range(1, feats)]
    outs = layer(behind, hidden, weights)
    done = [outs[0]] + [send(outs[step], "feat", step) for step in range(1, feats)]
    return gather_rows(behind, done)


def solution(mesh):
    return jax.shard_map(
        body,
        mesh=mesh,
        in_specs=(
            P(("blk", "sub"), "feat"),
            P(("blk", "sub"), None, None, None, None),
            P(("blk", "sub"), None, None),
            P(("blk", "sub"), None, None),
            P(("blk", "sub"), None),
            P(None, "feat"),
        ),
        out_specs=P(("blk", "sub"), "feat"),
        check_vma=False,
    )
```

time: 321 us -> 115 us (0.36)
  matrix products: 108 us -> 0 us
  local copies, waits for them, and re-layouts: 76 us -> 5.52 us
  waiting for transfers between devices: 120 us -> 52.2 us
  starting transfers between devices: 0.04 us -> 33.6 us
  Pallas kernels: 0 us -> 24.1 us
  between operations: 13.4 us -> 0.1 us
    dot_general x4 -> x0, matrix products: 108 us -> none  [the longest x1 55.4 us: one_piece(): jnp.einsum('sij,sjf->sif', adj_piece, selected, preferred_element_type=jn...]
    dot_general x2 -> x0, local copies, waits for them, and re-layouts: 76 us -> none  [the longest x1 66.9 us: one_piece(): jnp.einsum('sij,sjf->sif', adj_piece, selected, preferred_element_type=jn...]
    reduce_scatter x1 -> x0, waiting for transfers between devices: 74.1 us -> none  [body(): lax.psum_scatter(piece_terms.reshape(TGT_DEV * lax.axis_size(('blk', 'sub...]
    ppermute x0 -> x13, waiting for transfers between devices: none -> 52.2 us  [the longest x10 43 us: send(): lax.ppermute(value, axis, [(i, forward(i, step, size)) for i in range(siz...]
    all_gather x1 -> x0, waiting for transfers between devices: 46.4 us -> none  [body(): lax.all_gather(hidden, 'feat', axis=1, tiled=True)]
    ppermute x0 -> x13, starting transfers between devices: none -> 33.6 us  [the longest x10 25.8 us: send(): lax.ppermute(value, axis, [(i, forward(i, step, size)) for i in range(siz...]
    pallas_call x0 -> x6, Pallas kernels: none -> 24.1 us  [the longest x2 12 us: products(): pl.pallas_call(products_kernel, grid_spec=pltpu.PrefetchScalarGridSpec(nu...]
    unnamed x6 -> x38, local copies, waits for them, and re-layouts: 0.01 us -> 5.52 us
  transfers between devices with their start and end apart: 2 -> 13, of which waited for: 2 -> 7; matrix products, arithmetic and copies ran while one was open for 0% -> 1% of each run, Pallas kernels for 0% -> 7%
where the time goes in v1:
time: 115 us; the launch traced here: 116 us
  waiting for transfers between devices  52.2 us (45%)
  starting transfers between devices  33.6 us (29%)
  Pallas kernels  24.1 us (21%)
  local copies, waits for them, and re-layouts  5.52 us (5%)
    ppermute x10, waiting for transfers between devices, send(): lax.ppermute(value, axis, [(i, forward(i, step, size)) for i in range(siz...  43 us
    ppermute x10, starting transfers between devices, send(): lax.ppermute(value, axis, [(i, forward(i, step, size)) for i in range(siz...  25.8 us
    pallas_call x2, Pallas kernels, products(): pl.pallas_call(products_kernel, grid_spec=pltpu.PrefetchScalarGridSpec(nu...  12 us
    ppermute x3, waiting for transfers between devices, fetch(): lax.ppermute(value, axis, [(forward(i, step, size), i) for i in range(siz...  9.22 us
    ppermute x3, starting transfers between devices, fetch(): lax.ppermute(value, axis, [(forward(i, step, size), i) for i in range(siz...  7.79 us
    unnamed x38, local copies, waits for them, and re-layouts  5.52 us
    pallas_call x1, Pallas kernels, pair_sum(): pl.pallas_call(pair_sum_kernel, grid=(rows // tile,), in_specs=[pl.BlockS...  4.32 us
    pallas_call x1, Pallas kernels, layer(): pl.pallas_call(layer_kernel, in_specs=[pl.BlockSpec(memory_space=pltpu.SM...  3.15 us
  transfers between devices with their start and end apart: 13, of which 7 were waited for; matrix products, arithmetic and copies ran while one was open for 1% of the time, Pallas kernels for 7%

profile of v1, /device:TPU:0, one launch (start us, length us, event | category | flops | bytes accessed | tf_op | source)
XLA Modules:
  0.0 116.3 jit_solution(4189197970675443728)
XLA Ops:
  2.1 6.2 %products.3 = bf16[4,1024,256]{2,1,0:T(8,128)(2,1)S(1)} custom-call(s32[8,64]{1,0:T(8,128)S(1)} %bitcast.16, s32[8,64]{1,0:T(8,128)S(1)} %bitcast.18, s32[8]{0:T(128)S(1)} %bitcast.20, s32[4]{0:T(128)S(1)} %pad_add_fusion.2.ids, bf16[8192,256]{1,0:T(8,128)(2,1)} %src_hbm.3, bf16[8,64,128,128]{3,2,1,0:T(8,128)(2,1)} %bitcast.22), custom_call_target="tpu_custom_call" | custom-call | flops 2147483648 | bytes 12582912 | tf_op jit(solution)/shard_map/products/pallas_call | solution.py:84
  8.3 6.7 %collective-permute-start = (bf16[4,1024,256]{2,1,0:T(8,128)(2,1)S(1)}, bf16[4,1024,256]{2,1,0:T(8,128)(2,1)}, u32[]{:S(2)}, u32[]{:S(2)}) collective-permute-start(bf16[4,1024,256]{2,1,0:T(8,128)(2,1)S(1)} %products.3), channel_id=1, source_target_pairs={{0,4},{4,0},{1,5},{5,1},{2,6},{6,2},{3,7},{7,3},{8,12},{12,8},{9,1... | collective-permute-start | bytes 6291464 | tf_op jit(solution)/shard_map/ppermute | solution.py:29
  15.1 5.9 %products.2.own = bf16[4,1024,256]{2,1,0:T(8,128)(2,1)S(1)} custom-call(s32[8,64]{1,0:T(8,128)S(1)} %bitcast.17, s32[8,64]{1,0:T(8,128)S(1)} %bitcast.19, s32[8]{0:T(128)S(1)} %bitcast.21, s32[4]{0:T(128)S(1)} %pad_add_fusion.1.ids, bf16[8192,256]{1,0:T(8,128)(2,1)} %src_hbm.3, bf16[8,64,128,128]{3,2,1,0:T(8,128)(2,1)} %bitcast.23), custom_call_target="tpu_custom_call" | custom-call | flops 2147483648 | bytes 12582912 | tf_op jit(solution)/shard_map/products/pallas_call | solution.py:84
  20.9 1.3 %copy-done = bf16[4,1024,256]{2,1,0:T(8,128)(2,1)} copy-done((bf16[4,1024,256]{2,1,0:T(8,128)(2,1)}, bf16[4,1024,256]{2,1,0:T(8,128)(2,1)S(1)}, u32[]{:S(2)}) %copy-start) | copy-done | bytes 2097176
  22.3 4.3 %pair_sum.1 = (f32[1024,256]{1,0:T(8,128)}, bf16[1024,256]{1,0:T(8,128)(2,1)}, bf16[1024,256]{1,0:T(8,128)(2,1)}, bf16[1024,256]{1,0:T(8,128)(2,1)}) custom-call(bf16[4,1024,256]{2,1,0:T(8,128)(2,1)} %copy-done, bf16[4,1024,256]{2,1,0:T(8,128)(2,1)} %collective-permute-done.refs_0_), custom_call_target="tpu_custom_call" | custom-call | flops 1048576 | bytes 6291456 | tf_op jit(solution)/shard_map/pair_sum/pallas_call | solution.py:123
  26.6 7.8 %collective-permute-start.1 = (bf16[1024,256]{1,0:T(8,128)(2,1)}, bf16[1024,256]{1,0:T(8,128)(2,1)S(1)}, u32[]{:S(2)}, u32[]{:S(2)}) collective-permute-start(bf16[1024,256]{1,0:T(8,128)(2,1)} %get-tuple-element.18), channel_id=1, source_target_pairs={{0,8},{8,0},{16,24},{24,16},{1,9},{9,1},{17,25},{25,17},{2,10},{10... | collective-permute-start | bytes 1572872 | tf_op jit(solution)/shard_map/ppermute | solution.py:29
  34.5 1.4 %collective-permute-start.3 = (bf16[1024,256]{1,0:T(8,128)(2,1)}, bf16[1024,256]{1,0:T(8,128)(2,1)}, u32[]{:S(2)}, u32[]{:S(2)}) collective-permute-start(bf16[1024,256]{1,0:T(8,128)(2,1)} %get-tuple-element.20), channel_id=1, source_target_pairs={{0,24},{8,16},{16,8},{24,0},{1,25},{9,17},{17,9},{25,1},{2,26},{10... | collective-permute-start | bytes 1572872 | tf_op jit(solution)/shard_map/ppermute | solution.py:29
  35.9 1.6 %collective-permute-start.7 = (bf16[1024,256]{1,0:T(8,128)(2,1)S(1)}, bf16[1024,256]{1,0:T(8,128)(2,1)S(1)}, u32[]{:S(2)}, u32[]{:S(2)}) collective-permute-start(bf16[1024,256]{1,0:T(8,128)(2,1)S(1)} %copy-done.7), channel_id=1, source_target_pairs={{1,0},{0,1},{3,2},{2,3},{5,4},{4,5},{7,6},{6,7},{9,8},{8,9},{11,10... | collective-permute-start | bytes 1572872 | tf_op jit(solution)/shard_map/ppermute | solution.py:34
  37.5 2.6 %collective-permute-start.8 = (bf16[1024,256]{1,0:T(8,128)(2,1)S(1)}, bf16[1024,256]{1,0:T(8,128)(2,1)S(1)}, u32[]{:S(2)}, u32[]{:S(2)}) collective-permute-start(bf16[1024,256]{1,0:T(8,128)(2,1)S(1)} %copy-done.7), channel_id=1, source_target_pairs={{2,0},{3,1},{0,2},{1,3},{6,4},{7,5},{4,6},{5,7},{10,8},{11,9},{8,1... | collective-permute-start | bytes 1572872 | tf_op jit(solution)/shard_map/ppermute | solution.py:34
  40.1 7.2 %collective-permute-done.1.refs_0_ = bf16[1024,256]{1,0:T(8,128)(2,1)S(1)} collective-permute-done((bf16[1024,256]{1,0:T(8,128)(2,1)}, bf16[1024,256]{1,0:T(8,128)(2,1)S(1)}, u32[]{:S(2)}, u32[]{:S(2)}) %collective-permute-start.1) | collective-permute-done | bytes 524320 | tf_op jit(solution)/shard_map/ppermute | solution.py:29
  47.3 3.6 %collective-permute-start.9 = (bf16[1024,256]{1,0:T(8,128)(2,1)S(1)}, bf16[1024,256]{1,0:T(8,128)(2,1)S(1)}, u32[]{:S(2)}, u32[]{:S(2)}) collective-permute-start(bf16[1024,256]{1,0:T(8,128)(2,1)S(1)} %copy-done.7), channel_id=1, source_target_pairs={{3,0},{2,1},{1,2},{0,3},{7,4},{6,5},{5,6},{4,7},{11,8},{10,9},{9,1... | collective-permute-start | bytes 1572872 | tf_op jit(solution)/shard_map/ppermute | solution.py:34
  51.6 6.3 %collective-permute-done.2.refs_1_ = bf16[1024,256]{1,0:T(8,128)(2,1)S(1)} collective-permute-done((bf16[1024,256]{1,0:T(8,128)(2,1)}, bf16[1024,256]{1,0:T(8,128)(2,1)S(1)}, u32[]{:S(2)}, u32[]{:S(2)}) %collective-permute-start.2) | collective-permute-done | bytes 524320 | tf_op jit(solution)/shard_map/ppermute | solution.py:29
  58.6 2.6 %deal.1 = (bf16[256,256]{1,0:T(8,128)(2,1)}, bf16[256,256]{1,0:T(8,128)(2,1)}, bf16[256,256]{1,0:T(8,128)(2,1)}, bf16[256,256]{1,0:T(8,128)(2,1)}) custom-call(s32[4]{0:T(128)} %pad_add_fusion.places, f32[1024,256]{1,0:T(8,128)} %get-tuple-element.17.own, bf16[1024,256]{1,0:T(8,128)(2,1)} %copy-done.11, bf16[1024,256]{1,0:T(8,128)(2,1)} %copy-done.12, ...), custom_call_target="tpu_custom_call" | custom-call | flops 786432 | bytes 2621440 | tf_op jit(solution)/shard_map/deal/pallas_call | solution.py:155
  61.3 2.4 %collective-permute-start.4 = (bf16[256,256]{1,0:T(8,128)(2,1)}, bf16[256,256]{1,0:T(8,128)(2,1)S(1)}, u32[]{:S(2)}, u32[]{:S(2)}) collective-permute-start(bf16[256,256]{1,0:T(8,128)(2,1)} %get-tuple-element.22), channel_id=1, source_target_pairs={{0,1},{1,0},{2,3},{3,2},{4,5},{5,4},{6,7},{7,6},{8,9},{9,8},{10,11... | collective-permute-start | bytes 393224 | tf_op jit(solution)/shard_map/ppermute | solution.py:29
  63.7 2.6 %collective-permute-start.5 = (bf16[256,256]{1,0:T(8,128)(2,1)}, bf16[256,256]{1,0:T(8,128)(2,1)S(1)}, u32[]{:S(2)}, u32[]{:S(2)}) collective-permute-start(bf16[256,256]{1,0:T(8,128)(2,1)} %get-tuple-element.23), channel_id=1, source_target_pairs={{0,2},{1,3},{2,0},{3,1},{4,6},{5,7},{6,4},{7,5},{8,10},{9,11},{10,... | collective-permute-start | bytes 393224 | tf_op jit(solution)/shard_map/ppermute | solution.py:29
  66.3 9.2 %collective-permute-done.8.refs_6_ = bf16[1024,256]{1,0:T(8,128)(2,1)S(1)} collective-permute-done((bf16[1024,256]{1,0:T(8,128)(2,1)S(1)}, bf16[1024,256]{1,0:T(8,128)(2,1)S(1)}, u32[]{:S(2)}, u32[]{:S(2)}) %collective-permute-start.8) | collective-permute-done | bytes 524320 | tf_op jit(solution)/shard_map/ppermute | solution.py:34
  75.5 1.9 %collective-permute-done.4.refs_1_ = bf16[256,256]{1,0:T(8,128)(2,1)S(1)} collective-permute-done((bf16[256,256]{1,0:T(8,128)(2,1)}, bf16[256,256]{1,0:T(8,128)(2,1)S(1)}, u32[]{:S(2)}, u32[]{:S(2)}) %collective-permute-start.4) | collective-permute-done | bytes 131104 | tf_op jit(solution)/shard_map/ppermute | solution.py:29
  77.4 17.7 %collective-permute-done.5.refs_2_ = bf16[256,256]{1,0:T(8,128)(2,1)S(1)} collective-permute-done((bf16[256,256]{1,0:T(8,128)(2,1)}, bf16[256,256]{1,0:T(8,128)(2,1)S(1)}, u32[]{:S(2)}, u32[]{:S(2)}) %collective-permute-start.5) | collective-permute-done | bytes 131104 | tf_op jit(solution)/shard_map/ppermute | solution.py:29
  95.9 3.2 %layer.1 = (bf16[256,256]{1,0:T(8,128)(2,1)}, bf16[256,256]{1,0:T(8,128)(2,1)}, bf16[256,256]{1,0:T(8,128)(2,1)}, bf16[256,256]{1,0:T(8,128)(2,1)}) custom-call(s32[4]{0:T(128)} %pad_add_fusion.places, bf16[256,256]{1,0:T(8,128)(2,1)} %get-tuple-element.21.refs_0_, bf16[256,256]{1,0:T(8,128)(2,1)} %copy-done.13, bf16[256,256]{1,0:T(8,128)(2,1)} %copy-done.14, ...), custom_call_target="tpu_custom_call" | custom-call | flops 536870912 | bytes 2097152 | tf_op jit(solution)/shard_map/layer/pallas_call | solution.py:187
  99.0 2.4 %collective-permute-start.10 = (bf16[256,256]{1,0:T(8,128)(2,1)}, bf16[256,256]{1,0:T(8,128)(2,1)S(1)}, u32[]{:S(2)}, u32[]{:S(2)}) collective-permute-start(bf16[256,256]{1,0:T(8,128)(2,1)} %get-tuple-element.26), channel_id=1, source_target_pairs={{0,1},{1,0},{2,3},{3,2},{4,5},{5,4},{6,7},{7,6},{8,9},{9,8},{10,11... | collective-permute-start | bytes 393224 | tf_op jit(solution)/shard_map/ppermute | solution.py:29
  102.5 1.4 %collective-permute-start.12 = (bf16[256,256]{1,0:T(8,128)(2,1)}, bf16[256,256]{1,0:T(8,128)(2,1)S(1)}, u32[]{:S(2)}, u32[]{:S(2)}) collective-permute-start(bf16[256,256]{1,0:T(8,128)(2,1)} %get-tuple-element.28), channel_id=1, source_target_pairs={{0,3},{1,2},{2,1},{3,0},{4,7},{5,6},{6,5},{7,4},{8,11},{9,10},{10,... | collective-permute-start | bytes 393224 | tf_op jit(solution)/shard_map/ppermute | solution.py:29
  103.9 1.8 %collective-permute-done.10.refs_1_ = bf16[256,256]{1,0:T(8,128)(2,1)S(1)} collective-permute-done((bf16[256,256]{1,0:T(8,128)(2,1)}, bf16[256,256]{1,0:T(8,128)(2,1)S(1)}, u32[]{:S(2)}, u32[]{:S(2)}) %collective-permute-start.10) | collective-permute-done | bytes 131104 | tf_op jit(solution)/shard_map/ppermute | solution.py:29
  105.7 8.0 %collective-permute-done.11.refs_2_ = bf16[256,256]{1,0:T(8,128)(2,1)S(1)} collective-permute-done((bf16[256,256]{1,0:T(8,128)(2,1)}, bf16[256,256]{1,0:T(8,128)(2,1)S(1)}, u32[]{:S(2)}, u32[]{:S(2)}) %collective-permute-start.11) | collective-permute-done | bytes 131104 | tf_op jit(solution)/shard_map/ppermute | solution.py:29
  114.4 1.9 %gather_rows.1 = bf16[1024,256]{1,0:T(8,128)(2,1)} custom-call(s32[4]{0:T(128)} %pad_add_fusion.places, bf16[256,256]{1,0:T(8,128)(2,1)} %get-tuple-element.25.refs_0_, bf16[256,256]{1,0:T(8,128)(2,1)} %copy-done.16, bf16[256,256]{1,0:T(8,128)(2,1)} %copy-done.17, bf16[256,256]{1,0:T(8,128)(2,1)} %copy-done.18), custom_call_target="tpu_custom_call" | custom-call | tf_op jit(solution)/shard_map/gather_rows/pallas_call | solution.py:211
  (49 shorter events, 6.2 us)
Async XLA Ops:
  2.1 12.9 %copy-start.2 = (s32[1,8,64]{2,1,0:T(8,128)S(1)}, s32[1,8,64]{2,1,0:T(8,128)}, u32[]{:S(2)}) copy-start(s32[1,8,64]{2,1,0:T(8,128)} %param.8) | copy-start | bytes 6148
  2.1 12.9 %copy-start.4 = (s32[1,8,64]{2,1,0:T(8,128)S(1)}, s32[1,8,64]{2,1,0:T(8,128)}, u32[]{:S(2)}) copy-start(s32[1,8,64]{2,1,0:T(8,128)} %param.9) | copy-start | bytes 6148
  2.1 12.9 %copy-start.6 = (s32[1,8]{1,0:T(1,128)S(1)}, s32[1,8]{1,0:T(1,128)}, u32[]{:S(2)}) copy-start(s32[1,8]{1,0:T(1,128)} %param.10) | copy-start | bytes 100
  8.3 14.0 %collective-permute-start = (bf16[4,1024,256]{2,1,0:T(8,128)(2,1)S(1)}, bf16[4,1024,256]{2,1,0:T(8,128)(2,1)}, u32[]{:S(2)}, u32[]{:S(2)}) collective-permute-start(bf16[4,1024,256]{2,1,0:T(8,128)(2,1)S(1)} %products.3), channel_id=1, source_target_pairs={{0,4},{4,0},{1,5},{5,1},{2,6},{6,2},{3,7},{7,3},{8,12},{12,8},{9,1... | collective-permute-start | bytes 6291464 | tf_op jit(solution)/shard_map/ppermute | solution.py:29
  20.9 1.3 %copy-start = (bf16[4,1024,256]{2,1,0:T(8,128)(2,1)}, bf16[4,1024,256]{2,1,0:T(8,128)(2,1)S(1)}, u32[]{:S(2)}) copy-start(bf16[4,1024,256]{2,1,0:T(8,128)(2,1)S(1)} %products.2.own) | copy-start | bytes 6291460
  22.3 13.6 %copy-start.7 = (bf16[1024,256]{1,0:T(8,128)(2,1)S(1)}, bf16[1024,256]{1,0:T(8,128)(2,1)}, u32[]{:S(2)}) copy-start(bf16[1024,256]{1,0:T(8,128)(2,1)} %refs_4_.1) | copy-start | bytes 1572868
  26.6 20.7 %collective-permute-start.1 = (bf16[1024,256]{1,0:T(8,128)(2,1)}, bf16[1024,256]{1,0:T(8,128)(2,1)S(1)}, u32[]{:S(2)}, u32[]{:S(2)}) collective-permute-start(bf16[1024,256]{1,0:T(8,128)(2,1)} %get-tuple-element.18), channel_id=1, source_target_pairs={{0,8},{8,0},{16,24},{24,16},{1,9},{9,1},{17,25},{25,17},{2,10},{10... | collective-permute-start | bytes 1572872 | tf_op jit(solution)/shard_map/ppermute | solution.py:29
  34.3 23.5 %collective-permute-start.2 = (bf16[1024,256]{1,0:T(8,128)(2,1)}, bf16[1024,256]{1,0:T(8,128)(2,1)S(1)}, u32[]{:S(2)}, u32[]{:S(2)}) collective-permute-start(bf16[1024,256]{1,0:T(8,128)(2,1)} %get-tuple-element.19), channel_id=1, source_target_pairs={{0,16},{8,24},{16,0},{24,8},{1,17},{9,25},{17,1},{25,9},{2,18},{10... | collective-permute-start | bytes 1572872 | tf_op jit(solution)/shard_map/ppermute | solution.py:29
  34.5 23.4 %collective-permute-start.3 = (bf16[1024,256]{1,0:T(8,128)(2,1)}, bf16[1024,256]{1,0:T(8,128)(2,1)}, u32[]{:S(2)}, u32[]{:S(2)}) collective-permute-start(bf16[1024,256]{1,0:T(8,128)(2,1)} %get-tuple-element.20), channel_id=1, source_target_pairs={{0,24},{8,16},{16,8},{24,0},{1,25},{9,17},{17,9},{25,1},{2,26},{10... | collective-permute-start | bytes 1572872 | tf_op jit(solution)/shard_map/ppermute | solution.py:29
  35.9 30.4 %collective-permute-start.7 = (bf16[1024,256]{1,0:T(8,128)(2,1)S(1)}, bf16[1024,256]{1,0:T(8,128)(2,1)S(1)}, u32[]{:S(2)}, u32[]{:S(2)}) collective-permute-start(bf16[1024,256]{1,0:T(8,128)(2,1)S(1)} %copy-done.7), channel_id=1, source_target_pairs={{1,0},{0,1},{3,2},{2,3},{5,4},{4,5},{7,6},{6,7},{9,8},{8,9},{11,10... | collective-permute-start | bytes 1572872 | tf_op jit(solution)/shard_map/ppermute | solution.py:34
  37.5 38.0 %collective-permute-start.8 = (bf16[1024,256]{1,0:T(8,128)(2,1)S(1)}, bf16[1024,256]{1,0:T(8,128)(2,1)S(1)}, u32[]{:S(2)}, u32[]{:S(2)}) collective-permute-start(bf16[1024,256]{1,0:T(8,128)(2,1)S(1)} %copy-done.7), channel_id=1, source_target_pairs={{2,0},{3,1},{0,2},{1,3},{6,4},{7,5},{4,6},{5,7},{10,8},{11,9},{8,1... | collective-permute-start | bytes 1572872 | tf_op jit(solution)/shard_map/ppermute | solution.py:34
  47.3 10.5 %copy-start.11 = (bf16[1024,256]{1,0:T(8,128)(2,1)}, bf16[1024,256]{1,0:T(8,128)(2,1)S(1)}, u32[]{:S(2)}) copy-start(bf16[1024,256]{1,0:T(8,128)(2,1)S(1)} %collective-permute-done.1.refs_0_) | copy-start | bytes 1572868
  47.3 28.2 %collective-permute-start.9 = (bf16[1024,256]{1,0:T(8,128)(2,1)S(1)}, bf16[1024,256]{1,0:T(8,128)(2,1)S(1)}, u32[]{:S(2)}, u32[]{:S(2)}) collective-permute-start(bf16[1024,256]{1,0:T(8,128)(2,1)S(1)} %copy-done.7), channel_id=1, source_target_pairs={{3,0},{2,1},{1,2},{0,3},{7,4},{6,5},{5,6},{4,7},{11,8},{10,9},{9,1... | collective-permute-start | bytes 1572872 | tf_op jit(solution)/shard_map/ppermute | solution.py:34
  61.3 16.2 %collective-permute-start.4 = (bf16[256,256]{1,0:T(8,128)(2,1)}, bf16[256,256]{1,0:T(8,128)(2,1)S(1)}, u32[]{:S(2)}, u32[]{:S(2)}) collective-permute-start(bf16[256,256]{1,0:T(8,128)(2,1)} %get-tuple-element.22), channel_id=1, source_target_pairs={{0,1},{1,0},{2,3},{3,2},{4,5},{5,4},{6,7},{7,6},{8,9},{9,8},{10,11... | collective-permute-start | bytes 393224 | tf_op jit(solution)/shard_map/ppermute | solution.py:29
  63.7 31.5 %collective-permute-start.5 = (bf16[256,256]{1,0:T(8,128)(2,1)}, bf16[256,256]{1,0:T(8,128)(2,1)S(1)}, u32[]{:S(2)}, u32[]{:S(2)}) collective-permute-start(bf16[256,256]{1,0:T(8,128)(2,1)} %get-tuple-element.23), channel_id=1, source_target_pairs={{0,2},{1,3},{2,0},{3,1},{4,6},{5,7},{6,4},{7,5},{8,10},{9,11},{10,... | collective-permute-start | bytes 393224 | tf_op jit(solution)/shard_map/ppermute | solution.py:29
  66.3 28.9 %copy-start.8 = (bf16[1024,256]{1,0:T(8,128)(2,1)}, bf16[1024,256]{1,0:T(8,128)(2,1)S(1)}, u32[]{:S(2)}) copy-start(bf16[1024,256]{1,0:T(8,128)(2,1)S(1)} %collective-permute-done.7.refs_5_) | copy-start | bytes 1572868
  66.3 28.9 %collective-permute-start.6 = (bf16[256,256]{1,0:T(8,128)(2,1)}, bf16[256,256]{1,0:T(8,128)(2,1)S(1)}, u32[]{:S(2)}, u32[]{:S(2)}) collective-permute-start(bf16[256,256]{1,0:T(8,128)(2,1)} %get-tuple-element.24), channel_id=1, source_target_pairs={{0,3},{1,2},{2,1},{3,0},{4,7},{5,6},{6,5},{7,4},{8,11},{9,10},{10,... | collective-permute-start | bytes 393224 | tf_op jit(solution)/shard_map/ppermute | solution.py:29
  75.5 19.7 %copy-start.9 = (bf16[1024,256]{1,0:T(8,128)(2,1)}, bf16[1024,256]{1,0:T(8,128)(2,1)S(1)}, u32[]{:S(2)}) copy-start(bf16[1024,256]{1,0:T(8,128)(2,1)S(1)} %collective-permute-done.8.refs_6_) | copy-start | bytes 1572868
  75.5 19.7 %copy-start.10 = (bf16[1024,256]{1,0:T(8,128)(2,1)}, bf16[1024,256]{1,0:T(8,128)(2,1)S(1)}, u32[]{:S(2)}) copy-start(bf16[1024,256]{1,0:T(8,128)(2,1)S(1)} %collective-permute-done.9.refs_7_) | copy-start | bytes 1572868
  77.4 17.8 %copy-start.13 = (bf16[256,256]{1,0:T(8,128)(2,1)}, bf16[256,256]{1,0:T(8,128)(2,1)S(1)}, u32[]{:S(2)}) copy-start(bf16[256,256]{1,0:T(8,128)(2,1)S(1)} %collective-permute-done.4.refs_1_) | copy-start | bytes 393220
  99.0 6.6 %collective-permute-start.10 = (bf16[256,256]{1,0:T(8,128)(2,1)}, bf16[256,256]{1,0:T(8,128)(2,1)S(1)}, u32[]{:S(2)}, u32[]{:S(2)}) collective-permute-start(bf16[256,256]{1,0:T(8,128)(2,1)} %get-tuple-element.26), channel_id=1, source_target_pairs={{0,1},{1,0},{2,3},{3,2},{4,5},{5,4},{6,7},{7,6},{8,9},{9,8},{10,11... | collective-permute-start | bytes 393224 | tf_op jit(solution)/shard_map/ppermute | solution.py:29
  101.4 12.3 %collective-permute-start.11 = (bf16[256,256]{1,0:T(8,128)(2,1)}, bf16[256,256]{1,0:T(8,128)(2,1)S(1)}, u32[]{:S(2)}, u32[]{:S(2)}) collective-permute-start(bf16[256,256]{1,0:T(8,128)(2,1)} %get-tuple-element.27), channel_id=1, source_target_pairs={{0,2},{1,3},{2,0},{3,1},{4,6},{5,7},{6,4},{7,5},{8,10},{9,11},{10,... | collective-permute-start | bytes 393224 | tf_op jit(solution)/shard_map/ppermute | solution.py:29
  102.5 11.2 %collective-permute-start.12 = (bf16[256,256]{1,0:T(8,128)(2,1)}, bf16[256,256]{1,0:T(8,128)(2,1)S(1)}, u32[]{:S(2)}, u32[]{:S(2)}) collective-permute-start(bf16[256,256]{1,0:T(8,128)(2,1)} %get-tuple-element.28), channel_id=1, source_target_pairs={{0,3},{1,2},{2,1},{3,0},{4,7},{5,6},{6,5},{7,4},{8,11},{9,10},{10,... | collective-permute-start | bytes 393224 | tf_op jit(solution)/shard_map/ppermute | solution.py:29
  105.7 8.0 %copy-start.16 = (bf16[256,256]{1,0:T(8,128)(2,1)}, bf16[256,256]{1,0:T(8,128)(2,1)S(1)}, u32[]{:S(2)}) copy-start(bf16[256,256]{1,0:T(8,128)(2,1)S(1)} %collective-permute-done.10.refs_1_) | copy-start | bytes 393220
  (8 other events, 5.5 us)

commit v2 on v1

--- a/solution.py
+++ b/solution.py
@@ -9,7 +9,8 @@
 
 TGT_DEV = 1024
 GROUP = 8
-VMEM_BYTES = 48 * 2**20
+PRODUCTS_VMEM = 54 * 2**20
+SMALL_VMEM = 10 * 2**20
 
 
 def forward(index, step, size):
@@ -77,7 +78,7 @@
         out[0, row * block : (row + 1) * block, :] = acc[row].astype(out.dtype)
 
 
-def products(sources, adjacency, target, source, count, ids):
+def products(sources, adjacency, target, source, count, ids, dtype):
     _, slots, block, _ = adjacency.shape
     pieces = ids.shape[0]
     feat = sources.shape[1]
@@ -86,7 +87,7 @@
         grid_spec=pltpu.PrefetchScalarGridSpec(
             num_scalar_prefetch=4,
             grid=(pieces,),
-            in_specs=[pl.BlockSpec(memory_space=pl.ANY)] * 2,
+            in_specs=[pl.BlockSpec(memory_space=pltpu.HBM)] * 2,
             out_specs=pl.BlockSpec((1, TGT_DEV, feat), lambda step, *_: (step, 0, 0)),
             scratch_shapes=[
                 pltpu.VMEM(sources.shape, sources.dtype),
@@ -96,8 +97,8 @@
                 pltpu.SemaphoreType.DMA((pieces, slots // GROUP)),
             ],
         ),
-        out_shape=jax.ShapeDtypeStruct((pieces, TGT_DEV, feat), jnp.bfloat16),
-        compiler_params=pltpu.CompilerParams(vmem_limit_bytes=VMEM_BYTES),
+        out_shape=jax.ShapeDtypeStruct((pieces, TGT_DEV, feat), dtype),
+        compiler_params=pltpu.CompilerParams(vmem_limit_bytes=PRODUCTS_VMEM),
         cost_estimate=pl.CostEstimate(
             flops=2 * pieces * slots * block * block * feat,
             bytes_accessed=2 * (sources.size + pieces * slots * block * block),
@@ -119,16 +120,16 @@
 
 def pair_sum(own, others):
     parts, rows, feat = own.shape
-    tile = rows // 4
+    vmem = pl.BlockSpec(memory_space=pltpu.VMEM)
     return pl.pallas_call(
         pair_sum_kernel,
-        grid=(rows // tile,),
-        in_specs=[pl.BlockSpec((parts, tile, feat), lambda i: (0, i, 0))] * (1 + len(others)),
-        out_specs=[pl.BlockSpec((tile, feat), lambda i: (i, 0))] * parts,
+        in_specs=[vmem] * (1 + len(others)),
+        out_specs=[vmem] * parts,
         out_shape=[
             jax.ShapeDtypeStruct((rows, feat), jnp.float32 if part == 0 else jnp.bfloat16)
             for part in range(parts)
         ],
+        compiler_params=pltpu.CompilerParams(vmem_limit_bytes=SMALL_VMEM),
         cost_estimate=pl.CostEstimate(
             flops=own.size * len(others), bytes_accessed=6 * own.size, transcendentals=0
         ),
@@ -157,6 +158,7 @@
         in_specs=[pl.BlockSpec(memory_space=pltpu.SMEM)] + [vmem] * (1 + len(others)),
         out_specs=[vmem] * quarters,
         out_shape=[jax.ShapeDtypeStruct((rows // quarters, feat), jnp.bfloat16)] * quarters,
+        compiler_params=pltpu.CompilerParams(vmem_limit_bytes=SMALL_VMEM),
         cost_estimate=pl.CostEstimate(
             flops=own.size * len(others), bytes_accessed=10 * own.size, transcendentals=0
         ),
@@ -164,31 +166,47 @@
     )(places, own, *others)
 
 
-def layer_kernel(places, *refs):
-    parts = places.shape[0]
-    hidden, weights, outs = refs[:parts], refs[parts : 2 * parts], refs[2 * parts :]
-    depth = hidden[0].shape[1]
+def layer_kernel(shares, places, *refs):
+    parts = places.shape[0] // 2
+    count = 1 + (parts - 1) * shares
+    hidden, weights = refs[:parts], refs[parts : parts + count]
+    outs, held = refs[parts + count : -1], refs[-1]
+    depth = held.shape[2]
     for part in range(parts):
+        held[places[part]] = hidden[part][...]
+
+    def multiply(first, ref):
         total = None
-        for inner in range(parts):
-            rows = pl.ds(pl.multiple_of(places[inner] * depth, depth), depth)
-            term = jnp.dot(
-                hidden[inner][...], weights[part][rows, :], preferred_element_type=jnp.float32
-            )
+        for inner in range(ref.shape[0] // depth):
+            rows = ref[inner * depth : (inner + 1) * depth, :]
+            term = jnp.dot(held[first + inner], rows, preferred_element_type=jnp.float32)
             total = term if total is None else total + term
+        return total
+
+    for part in range(parts):
+        if part == 0:
+            total = multiply(0, weights[0])
+        else:
+            total = None
+            for share in range(shares):
+                ref = weights[1 + (part - 1) * shares + share]
+                term = multiply(places[parts + share] * (parts // shares), ref)
+                total = term if total is None else total + term
         outs[part][...] = jnp.maximum(total, 0.0).astype(outs[part].dtype)
 
 
-def layer(places, hidden, weights):
+def layer(places, hidden, weights, shares):
     parts = len(hidden)
-    rows = hidden[0].shape[0]
+    rows, feat = hidden[0].shape
     depth, columns = weights[0].shape
     vmem = pl.BlockSpec(memory_space=pltpu.VMEM)
     return pl.pallas_call(
-        layer_kernel,
-        in_specs=[pl.BlockSpec(memory_space=pltpu.SMEM)] + [vmem] * (2 * parts),
+        functools.partial(layer_kernel, shares),
+        in_specs=[pl.BlockSpec(memory_space=pltpu.SMEM)] + [vmem] * (parts + len(weights)),
         out_specs=[vmem] * parts,
         out_shape=[jax.ShapeDtypeStruct((rows, columns), jnp.bfloat16)] * parts,
+        scratch_shapes=[pltpu.VMEM((parts, rows, feat), jnp.bfloat16)],
+        compiler_params=pltpu.CompilerParams(vmem_limit_bytes=SMALL_VMEM),
         cost_estimate=pl.CostEstimate(
             flops=2 * rows * depth * columns * parts,
             bytes_accessed=2 * parts * depth * columns,
@@ -213,6 +231,7 @@
         in_specs=[pl.BlockSpec(memory_space=pltpu.SMEM)] + [vmem] * len(pieces),
         out_specs=vmem,
         out_shape=jax.ShapeDtypeStruct((rows * len(pieces), columns), pieces[0].dtype),
+        compiler_params=pltpu.CompilerParams(vmem_limit_bytes=SMALL_VMEM),
         name="gather_rows",
     )(places, *pieces)
 
@@ -221,24 +240,37 @@
     blks, subs, feats = (lax.axis_size(axis) for axis in ("blk", "sub", "feat"))
     blk, sub, feat = (lax.axis_index(axis) for axis in ("blk", "sub", "feat"))
 
-    def local(step):
+    def local(step, dtype):
         ids = jnp.stack(
             [forward(blk, part, blks) * subs + forward(sub, step, subs) for part in range(blks)]
         ).astype(jnp.int32)
         return products(
-            sources, adjacency[0], target_block[0], source_block[0], slot_counts[0], ids
+            sources, adjacency[0], target_block[0], source_block[0], slot_counts[0], ids, dtype
         )
 
-    weights = [weight] + [fetch(weight, "feat", step) for step in range(1, feats)]
-    arrived = [send(local(step), "sub", step) for step in range(1, subs)]
-    chip = pair_sum(local(0), arrived)
-    others = [send(chip[step], "blk", step) for step in range(1, blks)]
+    def exchange(parts, axis):
+        size = lax.axis_size(axis)
+        got = {step: send(parts[step], axis, step) for step in reversed(range(1, size))}
+        return [got[step] for step in range(1, size)]
+
+    share_rows = weight.shape[0] // subs
+    share = lax.dynamic_slice_in_dim(weight, sub * share_rows, share_rows, 0)
+
+    arrived = [send(local(step, jnp.bfloat16), "sub", step) for step in range(1, subs)]
+    chip = pair_sum(local(0, jnp.float32), arrived)
+    *chip, share = lax.optimization_barrier((*chip, share))
+    others = exchange(chip, "blk")
+    shares = [fetch(share, "feat", step) for step in range(1, feats)]
     ahead = jnp.stack([forward(feat, step, feats) for step in range(feats)]).astype(jnp.int32)
     behind = jnp.stack([backward(feat, step, feats) for step in range(feats)]).astype(jnp.int32)
+    turns = jnp.stack([forward(sub, step, subs) for step in range(subs)]).astype(jnp.int32)
     dealt = deal(ahead, chip[0], others)
-    hidden = [dealt[0]] + [send(dealt[step], "feat", step) for step in range(1, feats)]
-    outs = layer(behind, hidden, weights)
-    done = [outs[0]] + [send(outs[step], "feat", step) for step in range(1, feats)]
+    hidden = [dealt[0]] + exchange(dealt, "feat")
+    weights = [weight]
+    for part in shares:
+        weights += [part] + [fetch(part, "sub", step) for step in range(1, subs)]
+    outs = layer(jnp.concatenate([behind, behind * 0 + jnp.resize(turns, feats)]), hidden, weights, subs)
+    done = [outs[0]] + exchange(outs, "feat")
     return gather_rows(behind, done)
 
 

time: 115 us -> 88.4 us (0.77)
  waiting for transfers between devices: 52.2 us -> 37.2 us
  starting transfers between devices: 33.6 us -> 25.8 us
  Pallas kernels: 24.1 us -> 20.5 us
    ppermute x10, waiting for transfers between devices: 43 us -> 19.5 us  [send(): lax.ppermute(value, axis, [(i, forward(i, step, size)) for i in range(siz...]
    ppermute x3 -> x6, waiting for transfers between devices: 9.22 us -> 17.8 us  [fetch(): lax.ppermute(value, axis, [(forward(i, step, size), i) for i in range(siz...]
    ppermute x10, starting transfers between devices: 25.8 us -> 17.8 us  [send(): lax.ppermute(value, axis, [(i, forward(i, step, size)) for i in range(siz...]
    pallas_call x2, Pallas kernels: 7.47 us -> 2.93 us  [the longest x1 1.69 us: layer(): pl.pallas_call(functools.partial(layer_kernel, shares), in_specs=[pl.Bloc...]
    pallas_call x2, Pallas kernels: 12 us -> 14.8 us  [products(): pl.pallas_call(products_kernel, grid_spec=pltpu.PrefetchScalarGridSpec(nu...]
    pallas_call x1, Pallas kernels: 2.64 us -> 1.4 us  [deal(): pl.pallas_call(deal_kernel, in_specs=[pl.BlockSpec(memory_space=pltpu.SME...]
    unnamed x38 -> x8, local copies, waits for them, and re-layouts: 5.52 us -> 4.41 us
    ppermute x3 -> x6, starting transfers between devices: 7.79 us -> 8.06 us  [fetch(): lax.ppermute(value, axis, [(forward(i, step, size), i) for i in range(siz...]
  transfers between devices with their start and end apart: 13 -> 16, of which waited for: 7 -> 6; matrix products, arithmetic and copies ran while one was open for 1% -> 1% of each run, Pallas kernels for 7% -> 10%
where the time goes in v2:
time: 88.4 us; the launch traced here: 89.7 us
  waiting for transfers between devices  37.2 us (42%)
  starting transfers between devices  25.8 us (29%)
  Pallas kernels  20.5 us (23%)
  local copies, waits for them, and re-layouts  4.6 us (5%)
  other arithmetic  1.38 us (2%)
    ppermute x10, waiting for transfers between devices, send(): lax.ppermute(value, axis, [(i, forward(i, step, size)) for i in range(siz...  19.5 us
    ppermute x10, starting transfers between devices, send(): lax.ppermute(value, axis, [(i, forward(i, step, size)) for i in range(siz...  17.8 us
    ppermute x6, waiting for transfers between devices, fetch(): lax.ppermute(value, axis, [(forward(i, step, size), i) for i in range(siz...  17.8 us
    pallas_call x2, Pallas kernels, products(): pl.pallas_call(products_kernel, grid_spec=pltpu.PrefetchScalarGridSpec(nu...  14.8 us
    ppermute x6, starting transfers between devices, fetch(): lax.ppermute(value, axis, [(forward(i, step, size), i) for i in range(siz...  8.06 us
    unnamed x8, local copies, waits for them, and re-layouts  4.41 us
  transfers between devices with their start and end apart: 16, of which 6 were waited for; matrix products, arithmetic and copies ran while one was open for 1% of the time, Pallas kernels for 10%

profile of v2, /device:TPU:0, one launch (start us, length us, event | category | flops | bytes accessed | tf_op | source)
XLA Modules:
  0.0 89.7 jit_solution(7747140799586647555)
XLA Ops:
  0.6 7.3 %products.3 = bf16[4,1024,256]{2,1,0:T(8,128)(2,1)} custom-call(s32[8,64]{1,0:T(8,128)} %bitcast.20, s32[8,64]{1,0:T(8,128)} %bitcast.22, s32[8]{0:T(128)} %bitcast.24, s32[4]{0:T(128)} %pad_add_fusion.3.ids, bf16[8192,256]{1,0:T(8,128)(2,1)} %src_hbm.3, bf16[8,64,128,128]{3,2,1,0:T(8,128)(2,1)} %bitcast.18), custom_call_target="tpu_custom_call" | custom-call | flops 2147483648 | bytes 12582912 | tf_op jit(solution)/shard_map/products/pallas_call | solution.py:85
  7.9 3.6 %collective-permute-start = (bf16[4,1024,256]{2,1,0:T(8,128)(2,1)}, bf16[4,1024,256]{2,1,0:T(8,128)(2,1)S(1)}, u32[]{:S(2)}, u32[]{:S(2)}) collective-permute-start(bf16[4,1024,256]{2,1,0:T(8,128)(2,1)} %products.3), channel_id=1, source_target_pairs={{0,4},{4,0},{1,5},{5,1},{2,6},{6,2},{3,7},{7,3},{8,12},{12,8},{9,1... | collective-permute-start | bytes 6291464 | tf_op jit(solution)/shard_map/ppermute | solution.py:30
  12.1 7.5 %products.2.own = f32[4,1024,256]{2,1,0:T(8,128)} custom-call(s32[8,64]{1,0:T(8,128)} %bitcast.21, s32[8,64]{1,0:T(8,128)} %bitcast.23, s32[8]{0:T(128)} %bitcast.25, s32[4]{0:T(128)} %pad_add_fusion.2.ids, bf16[8192,256]{1,0:T(8,128)(2,1)} %src_hbm.3, bf16[8,64,128,128]{3,2,1,0:T(8,128)(2,1)} %bitcast.19), custom_call_target="tpu_custom_call" | custom-call | flops 2147483648 | bytes 12582912 | tf_op jit(solution)/shard_map/products/pallas_call | solution.py:85
  19.7 2.2 %copy-done = f32[4,1024,256]{2,1,0:T(8,128)S(1)} copy-done((f32[4,1024,256]{2,1,0:T(8,128)S(1)}, f32[4,1024,256]{2,1,0:T(8,128)}, u32[]{:S(2)}) %copy-start) | copy-done | bytes 4194328
  21.9 1.2 %pair_sum.1 = (f32[1024,256]{1,0:T(8,128)S(1)}, bf16[1024,256]{1,0:T(8,128)(2,1)S(1)}, bf16[1024,256]{1,0:T(8,128)(2,1)}, bf16[1024,256]{1,0:T(8,128)(2,1)}) custom-call(f32[4,1024,256]{2,1,0:T(8,128)S(1)} %copy-done, bf16[4,1024,256]{2,1,0:T(8,128)(2,1)S(1)} %collective-permute-done.refs_0_), custom_call_target="tpu_custom_call" | custom-call | flops 1048576 | bytes 6291456 | tf_op jit(solution)/shard_map/pair_sum/pallas_call | solution.py:124
  24.1 3.4 %collective-permute-start.9 = (bf16[512,256]{1,0:T(8,128)(2,1)S(1)}, bf16[512,256]{1,0:T(8,128)(2,1)S(1)}, u32[]{:S(2)}, u32[]{:S(2)}) collective-permute-start(bf16[512,256]{1,0:T(8,128)(2,1)S(1)} %constant_dynamic-slice_fusion), channel_id=1, source_target_pairs={{2,0},{3,1},{0,2},{1,3},{6,4},{7,5},{4,6},{5,7},{10,8},{11,9},{8,1... | collective-permute-start | bytes 786440 | tf_op jit(solution)/shard_map/ppermute | solution.py:35
  27.6 4.3 %collective-permute-start.2 = (bf16[1024,256]{1,0:T(8,128)(2,1)}, bf16[1024,256]{1,0:T(8,128)(2,1)S(1)}, u32[]{:S(2)}, u32[]{:S(2)}) collective-permute-start(bf16[1024,256]{1,0:T(8,128)(2,1)} %get-tuple-element.28), channel_id=1, source_target_pairs={{0,16},{8,24},{16,0},{24,8},{1,17},{9,25},{17,1},{25,9},{2,18},{10... | collective-permute-start | bytes 1572872 | tf_op jit(solution)/shard_map/ppermute | solution.py:30
  31.8 1.3 %collective-permute-start.11 = (bf16[512,256]{1,0:T(8,128)(2,1)S(1)}, bf16[512,256]{1,0:T(8,128)(2,1)S(1)}, u32[]{:S(2)}, u32[]{:S(2)}) collective-permute-start(bf16[512,256]{1,0:T(8,128)(2,1)S(1)} %constant_dynamic-slice_fusion), channel_id=1, source_target_pairs={{3,0},{2,1},{1,2},{0,3},{7,4},{6,5},{5,6},{4,7},{11,8},{10,9},{9,1... | collective-permute-start | bytes 786440 | tf_op jit(solution)/shard_map/ppermute | solution.py:35
  33.2 11.8 %collective-permute-done.9.refs_7_ = bf16[512,256]{1,0:T(8,128)(2,1)S(1)} collective-permute-done((bf16[512,256]{1,0:T(8,128)(2,1)S(1)}, bf16[512,256]{1,0:T(8,128)(2,1)S(1)}, u32[]{:S(2)}, u32[]{:S(2)}) %collective-permute-start.9) | collective-permute-done | bytes 262176 | tf_op jit(solution)/shard_map/ppermute | solution.py:35
  44.9 2.0 %collective-permute-start.7 = (bf16[512,256]{1,0:T(8,128)(2,1)S(1)}, bf16[512,256]{1,0:T(8,128)(2,1)S(1)}, u32[]{:S(2)}, u32[]{:S(2)}) collective-permute-start(bf16[512,256]{1,0:T(8,128)(2,1)S(1)} %constant_dynamic-slice_fusion), channel_id=1, source_target_pairs={{1,0},{0,1},{3,2},{2,3},{5,4},{4,5},{7,6},{6,7},{9,8},{8,9},{11,10... | collective-permute-start | bytes 786440 | tf_op jit(solution)/shard_map/ppermute | solution.py:35
  47.1 6.0 %collective-permute-done.7.refs_5_ = bf16[512,256]{1,0:T(8,128)(2,1)S(1)} collective-permute-done((bf16[512,256]{1,0:T(8,128)(2,1)S(1)}, bf16[512,256]{1,0:T(8,128)(2,1)S(1)}, u32[]{:S(2)}, u32[]{:S(2)}) %collective-permute-start.7) | collective-permute-done | bytes 262176 | tf_op jit(solution)/shard_map/ppermute | solution.py:35
  53.1 1.1 %collective-permute-start.12 = (bf16[512,256]{1,0:T(8,128)(2,1)S(1)}, bf16[512,256]{1,0:T(8,128)(2,1)S(1)}, u32[]{:S(2)}, u32[]{:S(2)}) collective-permute-start(bf16[512,256]{1,0:T(8,128)(2,1)S(1)} %collective-permute-done.11.refs_9_), channel_id=1, source_target_pairs={{4,0},{0,4},{5,1},{1,5},{6,2},{2,6},{7,3},{3,7},{12,8},{8,12},{13,... | collective-permute-start | bytes 786440 | tf_op jit(solution)/shard_map/ppermute | solution.py:35
  54.3 1.2 %copy-done.3 = f32[1024,256]{1,0:T(8,128)S(1)} copy-done((f32[1024,256]{1,0:T(8,128)S(1)}, f32[1024,256]{1,0:T(8,128)}, u32[]{:S(2)}) %copy-start.3) | copy-done | bytes 1048600
  55.5 1.4 %deal.1 = (bf16[256,256]{1,0:T(8,128)(2,1)S(1)}, bf16[256,256]{1,0:T(8,128)(2,1)}, bf16[256,256]{1,0:T(8,128)(2,1)}, bf16[256,256]{1,0:T(8,128)(2,1)}) custom-call(s32[4]{0:T(128)S(1)} %pad_add_fusion.places, f32[1024,256]{1,0:T(8,128)S(1)} %copy-done.3, bf16[1024,256]{1,0:T(8,128)(2,1)S(1)} %collective-permute-done.1.refs_0_, ...), custom_call_target="tpu_custom_call" | custom-call | flops 786432 | bytes 2621440 | tf_op jit(solution)/shard_map/deal/pallas_call | solution.py:156
  56.9 1.9 %collective-permute-start.4 = (bf16[256,256]{1,0:T(8,128)(2,1)}, bf16[256,256]{1,0:T(8,128)(2,1)S(1)}, u32[]{:S(2)}, u32[]{:S(2)}) collective-permute-start(bf16[256,256]{1,0:T(8,128)(2,1)} %get-tuple-element.31), channel_id=1, source_target_pairs={{0,1},{1,0},{2,3},{3,2},{4,5},{5,4},{6,7},{7,6},{8,9},{9,8},{10,11... | collective-permute-start | bytes 393224 | tf_op jit(solution)/shard_map/ppermute | solution.py:30
  58.8 3.1 %collective-permute-start.5 = (bf16[256,256]{1,0:T(8,128)(2,1)}, bf16[256,256]{1,0:T(8,128)(2,1)S(1)}, u32[]{:S(2)}, u32[]{:S(2)}) collective-permute-start(bf16[256,256]{1,0:T(8,128)(2,1)} %get-tuple-element.32), channel_id=1, source_target_pairs={{0,2},{1,3},{2,0},{3,1},{4,6},{5,7},{6,4},{7,5},{8,10},{9,11},{10,... | collective-permute-start | bytes 393224 | tf_op jit(solution)/shard_map/ppermute | solution.py:30
  62.2 2.6 %collective-permute-done.4.refs_1_ = bf16[256,256]{1,0:T(8,128)(2,1)S(1)} collective-permute-done((bf16[256,256]{1,0:T(8,128)(2,1)}, bf16[256,256]{1,0:T(8,128)(2,1)S(1)}, u32[]{:S(2)}, u32[]{:S(2)}) %collective-permute-start.4) | collective-permute-done | bytes 131104 | tf_op jit(solution)/shard_map/ppermute | solution.py:30
  64.8 7.3 %collective-permute-done.5.refs_2_ = bf16[256,256]{1,0:T(8,128)(2,1)S(1)} collective-permute-done((bf16[256,256]{1,0:T(8,128)(2,1)}, bf16[256,256]{1,0:T(8,128)(2,1)S(1)}, u32[]{:S(2)}, u32[]{:S(2)}) %collective-permute-start.5) | collective-permute-done | bytes 131104 | tf_op jit(solution)/shard_map/ppermute | solution.py:30
  72.2 1.7 %layer.1 = (bf16[256,256]{1,0:T(8,128)(2,1)S(1)}, bf16[256,256]{1,0:T(8,128)(2,1)S(1)}, bf16[256,256]{1,0:T(8,128)(2,1)S(1)}, bf16[256,256]{1,0:T(8,128)(2,1)S(1)}) custom-call(s32[8]{0:T(128)S(1)} %concatenate.4.places, bf16[256,256]{1,0:T(8,128)(2,1)S(1)} %get-tuple-element.30.refs_0_, bf16[256,256]{1,0:T(8,128)(2,1)S(1)} %collective-permute-done.4.refs_1_, ...), custom_call_target="tpu_custom_call" | custom-call | flops 536870912 | bytes 2097152 | tf_op jit(solution)/shard_map/layer/pallas_call | solution.py:203
  73.9 2.5 %collective-permute-start.13 = (bf16[256,256]{1,0:T(8,128)(2,1)S(1)}, bf16[256,256]{1,0:T(8,128)(2,1)S(1)}, u32[]{:S(2)}, u32[]{:S(2)}) collective-permute-start(bf16[256,256]{1,0:T(8,128)(2,1)S(1)} %get-tuple-element.36), channel_id=1, source_target_pairs={{0,1},{1,0},{2,3},{3,2},{4,5},{5,4},{6,7},{7,6},{8,9},{9,8},{10,11... | collective-permute-start | bytes 393224 | tf_op jit(solution)/shard_map/ppermute | solution.py:30
  77.3 1.5 %collective-permute-start.15 = (bf16[256,256]{1,0:T(8,128)(2,1)S(1)}, bf16[256,256]{1,0:T(8,128)(2,1)S(1)}, u32[]{:S(2)}, u32[]{:S(2)}) collective-permute-start(bf16[256,256]{1,0:T(8,128)(2,1)S(1)} %get-tuple-element.38), channel_id=1, source_target_pairs={{0,3},{1,2},{2,1},{3,0},{4,7},{5,6},{6,5},{7,4},{8,11},{9,10},{10,... | collective-permute-start | bytes 393224 | tf_op jit(solution)/shard_map/ppermute | solution.py:30
  78.8 1.5 %collective-permute-done.13.refs_1_ = bf16[256,256]{1,0:T(8,128)(2,1)S(1)} collective-permute-done((bf16[256,256]{1,0:T(8,128)(2,1)S(1)}, bf16[256,256]{1,0:T(8,128)(2,1)S(1)}, u32[]{:S(2)}, u32[]{:S(2)}) %collective-permute-start.13) | collective-permute-done | bytes 131104 | tf_op jit(solution)/shard_map/ppermute | solution.py:30
  80.3 8.0 %collective-permute-done.14.refs_2_ = bf16[256,256]{1,0:T(8,128)(2,1)S(1)} collective-permute-done((bf16[256,256]{1,0:T(8,128)(2,1)S(1)}, bf16[256,256]{1,0:T(8,128)(2,1)S(1)}, u32[]{:S(2)}, u32[]{:S(2)}) %collective-permute-start.14) | collective-permute-done | bytes 131104 | tf_op jit(solution)/shard_map/ppermute | solution.py:30
  88.3 1.4 %gather_rows.1 = bf16[1024,256]{1,0:T(8,128)(2,1)} custom-call(s32[4]{0:T(128)S(1)} %pad_add_fusion.places, bf16[256,256]{1,0:T(8,128)(2,1)S(1)} %get-tuple-element.35.refs_0_, bf16[256,256]{1,0:T(8,128)(2,1)S(1)} %collective-permute-done.13.refs_1_, bf16[256,256]{1,0:T(8,128)(2,1)S(1)} %collective-permute-done.14.refs_2_, ...), custom_call_target="tpu_custom_call" | custom-call | tf_op jit(solution)/shard_map/gather_rows/pallas_call | solution.py:229
  (30 shorter events, 3.8 us)
Async XLA Ops:
  0.6 11.5 %copy-start.1 = (bf16[1024,256]{1,0:T(8,128)(2,1)S(1)}, bf16[1024,256]{1,0:T(8,128)(2,1)}, u32[]{:S(2)}) copy-start(bf16[1024,256]{1,0:T(8,128)(2,1)} %refs_4_.1) | copy-start | bytes 1572868
  7.9 11.8 %collective-permute-start = (bf16[4,1024,256]{2,1,0:T(8,128)(2,1)}, bf16[4,1024,256]{2,1,0:T(8,128)(2,1)S(1)}, u32[]{:S(2)}, u32[]{:S(2)}) collective-permute-start(bf16[4,1024,256]{2,1,0:T(8,128)(2,1)} %products.3), channel_id=1, source_target_pairs={{0,4},{4,0},{1,5},{5,1},{2,6},{6,2},{3,7},{7,3},{8,12},{12,8},{9,1... | collective-permute-start | bytes 6291464 | tf_op jit(solution)/shard_map/ppermute | solution.py:30
  19.7 2.2 %copy-start = (f32[4,1024,256]{2,1,0:T(8,128)S(1)}, f32[4,1024,256]{2,1,0:T(8,128)}, u32[]{:S(2)}) copy-start(f32[4,1024,256]{2,1,0:T(8,128)} %products.2.own) | copy-start | bytes 12582916
  23.1 1.0 %copy-start.2 = (f32[1024,256]{1,0:T(8,128)}, f32[1024,256]{1,0:T(8,128)S(1)}, u32[]{:S(2)}) copy-start(f32[1024,256]{1,0:T(8,128)S(1)} %get-tuple-element.26.own) | copy-start | bytes 3145732
  24.1 20.8 %collective-permute-start.9 = (bf16[512,256]{1,0:T(8,128)(2,1)S(1)}, bf16[512,256]{1,0:T(8,128)(2,1)S(1)}, u32[]{:S(2)}, u32[]{:S(2)}) collective-permute-start(bf16[512,256]{1,0:T(8,128)(2,1)S(1)} %constant_dynamic-slice_fusion), channel_id=1, source_target_pairs={{2,0},{3,1},{0,2},{1,3},{6,4},{7,5},{4,6},{5,7},{10,8},{11,9},{8,1... | collective-permute-start | bytes 786440 | tf_op jit(solution)/shard_map/ppermute | solution.py:35
  27.6 26.7 %collective-permute-start.1 = (bf16[1024,256]{1,0:T(8,128)(2,1)S(1)}, bf16[1024,256]{1,0:T(8,128)(2,1)S(1)}, u32[]{:S(2)}, u32[]{:S(2)}) collective-permute-start(bf16[1024,256]{1,0:T(8,128)(2,1)S(1)} %get-tuple-element.27), channel_id=1, source_target_pairs={{0,8},{8,0},{16,24},{24,16},{1,9},{9,1},{17,25},{25,17},{2,10},{10... | collective-permute-start | bytes 1572872 | tf_op jit(solution)/shard_map/ppermute | solution.py:30
  27.6 26.7 %collective-permute-start.2 = (bf16[1024,256]{1,0:T(8,128)(2,1)}, bf16[1024,256]{1,0:T(8,128)(2,1)S(1)}, u32[]{:S(2)}, u32[]{:S(2)}) collective-permute-start(bf16[1024,256]{1,0:T(8,128)(2,1)} %get-tuple-element.28), channel_id=1, source_target_pairs={{0,16},{8,24},{16,0},{24,8},{1,17},{9,25},{17,1},{25,9},{2,18},{10... | collective-permute-start | bytes 1572872 | tf_op jit(solution)/shard_map/ppermute | solution.py:30
  31.8 22.5 %collective-permute-start.3 = (bf16[1024,256]{1,0:T(8,128)(2,1)}, bf16[1024,256]{1,0:T(8,128)(2,1)S(1)}, u32[]{:S(2)}, u32[]{:S(2)}) collective-permute-start(bf16[1024,256]{1,0:T(8,128)(2,1)} %get-tuple-element.29), channel_id=1, source_target_pairs={{0,24},{8,16},{16,8},{24,0},{1,25},{9,17},{17,9},{25,1},{2,26},{10... | collective-permute-start | bytes 1572872 | tf_op jit(solution)/shard_map/ppermute | solution.py:30
  31.8 15.1 %collective-permute-start.11 = (bf16[512,256]{1,0:T(8,128)(2,1)S(1)}, bf16[512,256]{1,0:T(8,128)(2,1)S(1)}, u32[]{:S(2)}, u32[]{:S(2)}) collective-permute-start(bf16[512,256]{1,0:T(8,128)(2,1)S(1)} %constant_dynamic-slice_fusion), channel_id=1, source_target_pairs={{3,0},{2,1},{1,2},{0,3},{7,4},{6,5},{5,6},{4,7},{11,8},{10,9},{9,1... | collective-permute-start | bytes 786440 | tf_op jit(solution)/shard_map/ppermute | solution.py:35
  44.9 8.2 %collective-permute-start.7 = (bf16[512,256]{1,0:T(8,128)(2,1)S(1)}, bf16[512,256]{1,0:T(8,128)(2,1)S(1)}, u32[]{:S(2)}, u32[]{:S(2)}) collective-permute-start(bf16[512,256]{1,0:T(8,128)(2,1)S(1)} %constant_dynamic-slice_fusion), channel_id=1, source_target_pairs={{1,0},{0,1},{3,2},{2,3},{5,4},{4,5},{7,6},{6,7},{9,8},{8,9},{11,10... | collective-permute-start | bytes 786440 | tf_op jit(solution)/shard_map/ppermute | solution.py:35
  46.9 15.1 %collective-permute-start.10 = (bf16[512,256]{1,0:T(8,128)(2,1)S(1)}, bf16[512,256]{1,0:T(8,128)(2,1)S(1)}, u32[]{:S(2)}, u32[]{:S(2)}) collective-permute-start(bf16[512,256]{1,0:T(8,128)(2,1)S(1)} %collective-permute-done.9.refs_7_), channel_id=1, source_target_pairs={{4,0},{0,4},{5,1},{1,5},{6,2},{2,6},{7,3},{3,7},{12,8},{8,12},{13,... | collective-permute-start | bytes 786440 | tf_op jit(solution)/shard_map/ppermute | solution.py:35
  53.1 9.1 %collective-permute-start.12 = (bf16[512,256]{1,0:T(8,128)(2,1)S(1)}, bf16[512,256]{1,0:T(8,128)(2,1)S(1)}, u32[]{:S(2)}, u32[]{:S(2)}) collective-permute-start(bf16[512,256]{1,0:T(8,128)(2,1)S(1)} %collective-permute-done.11.refs_9_), channel_id=1, source_target_pairs={{4,0},{0,4},{5,1},{1,5},{6,2},{2,6},{7,3},{3,7},{12,8},{8,12},{13,... | collective-permute-start | bytes 786440 | tf_op jit(solution)/shard_map/ppermute | solution.py:35
  54.2 8.0 %collective-permute-start.8 = (bf16[512,256]{1,0:T(8,128)(2,1)S(1)}, bf16[512,256]{1,0:T(8,128)(2,1)}, u32[]{:S(2)}, u32[]{:S(2)}) collective-permute-start(bf16[512,256]{1,0:T(8,128)(2,1)S(1)} %collective-permute-done.7.refs_5_), channel_id=1, source_target_pairs={{4,0},{0,4},{5,1},{1,5},{6,2},{2,6},{7,3},{3,7},{12,8},{8,12},{13,... | collective-permute-start | bytes 786440 | tf_op jit(solution)/shard_map/ppermute | solution.py:35
  54.3 1.2 %copy-start.3 = (f32[1024,256]{1,0:T(8,128)S(1)}, f32[1024,256]{1,0:T(8,128)}, u32[]{:S(2)}) copy-start(f32[1024,256]{1,0:T(8,128)} %copy-done.2) | copy-start | bytes 3145732
  56.9 7.9 %collective-permute-start.4 = (bf16[256,256]{1,0:T(8,128)(2,1)}, bf16[256,256]{1,0:T(8,128)(2,1)S(1)}, u32[]{:S(2)}, u32[]{:S(2)}) collective-permute-start(bf16[256,256]{1,0:T(8,128)(2,1)} %get-tuple-element.31), channel_id=1, source_target_pairs={{0,1},{1,0},{2,3},{3,2},{4,5},{5,4},{6,7},{7,6},{8,9},{9,8},{10,11... | collective-permute-start | bytes 393224 | tf_op jit(solution)/shard_map/ppermute | solution.py:30
  58.8 13.4 %collective-permute-start.5 = (bf16[256,256]{1,0:T(8,128)(2,1)}, bf16[256,256]{1,0:T(8,128)(2,1)S(1)}, u32[]{:S(2)}, u32[]{:S(2)}) collective-permute-start(bf16[256,256]{1,0:T(8,128)(2,1)} %get-tuple-element.32), channel_id=1, source_target_pairs={{0,2},{1,3},{2,0},{3,1},{4,6},{5,7},{6,4},{7,5},{8,10},{9,11},{10,... | collective-permute-start | bytes 393224 | tf_op jit(solution)/shard_map/ppermute | solution.py:30
  62.0 10.2 %collective-permute-start.6 = (bf16[256,256]{1,0:T(8,128)(2,1)}, bf16[256,256]{1,0:T(8,128)(2,1)S(1)}, u32[]{:S(2)}, u32[]{:S(2)}) collective-permute-start(bf16[256,256]{1,0:T(8,128)(2,1)} %get-tuple-element.33), channel_id=1, source_target_pairs={{0,3},{1,2},{2,1},{3,0},{4,7},{5,6},{6,5},{7,4},{8,11},{9,10},{10,... | collective-permute-start | bytes 393224 | tf_op jit(solution)/shard_map/ppermute | solution.py:30
  73.9 6.4 %collective-permute-start.13 = (bf16[256,256]{1,0:T(8,128)(2,1)S(1)}, bf16[256,256]{1,0:T(8,128)(2,1)S(1)}, u32[]{:S(2)}, u32[]{:S(2)}) collective-permute-start(bf16[256,256]{1,0:T(8,128)(2,1)S(1)} %get-tuple-element.36), channel_id=1, source_target_pairs={{0,1},{1,0},{2,3},{3,2},{4,5},{5,4},{6,7},{7,6},{8,9},{9,8},{10,11... | collective-permute-start | bytes 393224 | tf_op jit(solution)/shard_map/ppermute | solution.py:30
  76.3 12.0 %collective-permute-start.14 = (bf16[256,256]{1,0:T(8,128)(2,1)S(1)}, bf16[256,256]{1,0:T(8,128)(2,1)S(1)}, u32[]{:S(2)}, u32[]{:S(2)}) collective-permute-start(bf16[256,256]{1,0:T(8,128)(2,1)S(1)} %get-tuple-element.37), channel_id=1, source_target_pairs={{0,2},{1,3},{2,0},{3,1},{4,6},{5,7},{6,4},{7,5},{8,10},{9,11},{10,... | collective-permute-start | bytes 393224 | tf_op jit(solution)/shard_map/ppermute | solution.py:30
  77.3 11.0 %collective-permute-start.15 = (bf16[256,256]{1,0:T(8,128)(2,1)S(1)}, bf16[256,256]{1,0:T(8,128)(2,1)S(1)}, u32[]{:S(2)}, u32[]{:S(2)}) collective-permute-start(bf16[256,256]{1,0:T(8,128)(2,1)S(1)} %get-tuple-element.38), channel_id=1, source_target_pairs={{0,3},{1,2},{2,1},{3,0},{4,7},{5,6},{6,5},{7,4},{8,11},{9,10},{10,... | collective-permute-start | bytes 393224 | tf_op jit(solution)/shard_map/ppermute | solution.py:30

commit v3 on v0

v3 whole, which is shorter than its diff:
```python
import functools

import jax
import jax.numpy as jnp
from jax import lax
from jax.experimental import pallas as pl
from jax.experimental.pallas import tpu as pltpu
from jax.sharding import PartitionSpec as P

TGT_DEV = 1024
GROUP = 8
PAIRS = 8
PLAN_VMEM = 45 * 2**20
PRODUCTS_VMEM = 36 * 2**20
SMALL_VMEM = 10 * 2**20


def forward(index, step, size):
    if size & (size - 1) == 0:
        return index ^ step
    return (index + step) % size


def backward(index, step, size):
    if size & (size - 1) == 0:
        return index ^ step
    return (index + size - step) % size


def send(value, axis, step):
    size = lax.axis_size(axis)
    return lax.ppermute(value, axis, [(i, forward(i, step, size)) for i in range(size)])


def fetch(value, axis, step):
    size = lax.axis_size(axis)
    return lax.ppermute(value, axis, [(forward(i, step, size), i) for i in range(size)])


def plan_sizes(slots, targets, blocks):
    rows = -(-((slots + targets) // 2) // PAIRS) * PAIRS
    return rows, slots.bit_length(), (targets - 1).bit_length(), (blocks - 1).bit_length()


class Tiles:
    def __init__(self, adj, tiles, sem, numbers, counts):
        self.adj, self.tiles, self.sem = adj, tiles, sem
        self.numbers, self.counts = numbers, counts

    def copy(self, part, group):
        some = pl.ds(group * GROUP, GROUP)
        return pltpu.make_async_copy(
            self.adj.at[0, self.numbers[part], some],
            self.tiles.at[part, some],
            self.sem.at[part, group],
        )

    def each(self, act):
        for part, count in enumerate(self.counts):

            @pl.loop(0, (count + GROUP - 1) // GROUP)
            def _(group):
                act(self.copy(part, group))

    def start(self):
        self.each(lambda copy: copy.start())
        for part in range(len(self.counts)):
            zero = jnp.zeros(self.tiles.shape[2:], self.tiles.dtype)
            self.tiles[part, self.tiles.shape[1] - 1] = zero

    def wait(self):
        self.each(lambda copy: copy.wait())


def tiles_shape(adjacency, pieces):
    slots, block = adjacency.shape[2:4]
    return jax.ShapeDtypeStruct((pieces, slots + 1, block, block), adjacency.dtype)


def tiles_sems(adjacency, pieces):
    return pltpu.SemaphoreType.DMA((pieces, adjacency.shape[2] // GROUP))


def plan_kernel(
    targets, blocks, later, ids, count, target_hbm, source_hbm, src_hbm, adj_hbm, weight,
    out, src, tiles, share, target_ref, source_ref, sems, tile_sems,
):
    small = [
        pltpu.make_async_copy(target_hbm, target_ref, sems.at[0]),
        pltpu.make_async_copy(source_hbm, source_ref, sems.at[1]),
    ]
    large = pltpu.make_async_copy(src_hbm, src, sems.at[2])
    height = share.shape[0]
    mine = pl.ds(pl.multiple_of(ids[ids.shape[0] - 1] * height, height), height)
    part_copy = pltpu.make_async_copy(weight.at[mine], share, sems.at[3])
    part_copy.start()
    for copy in small:
        copy.start()
    large.start()
    numbers = [ids[place] for place in later]
    loads = Tiles(adj_hbm, tiles, tile_sems, numbers, [count[0, number] for number in numbers])
    loads.start()
    for copy in small:
        copy.wait()
    pieces, slots = target_ref.shape[1:]
    rows, slot_bits, target_bits, block_bits = plan_sizes(slots, targets, blocks)

    def iota(shape, axis):
        return lax.broadcasted_iota(jnp.int32, shape, axis)

    def exact(left, right):
        return jnp.dot(
            left.astype(jnp.bfloat16), right.astype(jnp.bfloat16), preferred_element_type=jnp.float32
        )

    lane = iota((1, slots), 1)
    hot, rest = [], []
    for part in range(pieces):
        piece = ids[part]
        live = lane < count[0, piece]
        target = target_ref[0, pl.ds(piece, 1), :]
        rest.append((live, target, source_ref[0, pl.ds(piece, 1), :]))
        hot.append(((iota((targets, slots), 0) == target) & live).astype(jnp.float32))
    every = jnp.concatenate(hot, axis=0)
    before = (iota((slots, slots), 0) < iota((slots, slots), 1)).astype(jnp.float32)
    order = exact(every, before).astype(jnp.int32)
    pairs = (jnp.sum(every, axis=1, keepdims=True).astype(jnp.int32) + 1) // 2
    size = pieces * targets
    above = (iota((size, size), 1) < iota((size, size), 0)) & (
        iota((size, size), 1) // targets == iota((size, size), 0) // targets
    )
    wide = jnp.broadcast_to(pairs.astype(jnp.float32), (size, slots))
    first = exact(above.astype(jnp.float32), wide).astype(jnp.int32)
    place = every * (first + order // 2).astype(jnp.float32)
    odd = every * (order % 2).astype(jnp.float32)

    column = iota((rows, pieces), 1)
    plan = jnp.zeros((rows, pieces), jnp.int32)
    extra = jnp.zeros((8, pieces), jnp.int32)
    small = iota((8, pieces), 0)
    for part in range(pieces):
        live, target, source = rest[part]
        mine = slice(part * targets, (part + 1) * targets)
        index = jnp.sum(place[mine], axis=0, keepdims=True).astype(jnp.int32)
        second = jnp.sum(odd[mine], axis=0, keepdims=True) > 0
        hit = (iota((rows, slots), 0) == index) & live
        code = (slots - lane) | (source << slot_bits)
        one = code | (target << (slot_bits + block_bits))
        one = jnp.where(hit & jnp.logical_not(second), one.astype(jnp.float32), 0.0)
        two = jnp.where(hit & second, code.astype(jnp.float32), 0.0)
        one = jnp.sum(one, axis=1, keepdims=True).astype(jnp.int32)
        two = jnp.sum(two, axis=1, keepdims=True).astype(jnp.int32)
        both = one | (two << (slot_bits + block_bits + target_bits))
        plan = jnp.where(column == part, both, plan)
        total = jnp.sum(pairs[mine].astype(jnp.float32), axis=0, keepdims=True).astype(jnp.int32)
        values = jnp.where(small == 0, total, jnp.where(small == 1, count[0, ids[part]], ids[part]))
        extra = jnp.where(iota((8, pieces), 1) == part, values, extra)
    out[0:rows, :] = plan
    out[rows:, :] = extra
    large.wait()
    loads.wait()
    part_copy.wait()


def make_plan(target_block, source_block, slot_counts, ids, sources, adjacency, weight, subs, later):
    _, pieces, slots = target_block.shape
    block = adjacency.shape[-1]
    targets, blocks = TGT_DEV // block, sources.shape[0] // block
    rows = plan_sizes(slots, targets, blocks)[0]
    smem, vmem, hbm = (
        pl.BlockSpec(memory_space=space) for space in (pltpu.SMEM, pltpu.VMEM, pltpu.HBM)
    )
    return pl.pallas_call(
        functools.partial(plan_kernel, targets, blocks, later),
        in_specs=[smem, smem] + [hbm] * 5,
        out_specs=[vmem] * 4,
        out_shape=[
            jax.ShapeDtypeStruct((rows + 8, pieces), jnp.int32),
            jax.ShapeDtypeStruct(sources.shape, sources.dtype),
            tiles_shape(adjacency, len(later)),
            jax.ShapeDtypeStruct((weight.shape[0] // subs, weight.shape[1]), weight.dtype),
        ],
        scratch_shapes=[
            pltpu.VMEM(target_block.shape, target_block.dtype),
            pltpu.VMEM(source_block.shape, source_block.dtype),
            pltpu.SemaphoreType.DMA((4,)),
            tiles_sems(adjacency, len(later)),
        ],
        compiler_params=pltpu.CompilerParams(vmem_limit_bytes=PLAN_VMEM),
        name="plan",
    )(ids, slot_counts, target_block, source_block, sources, adjacency, weight)


def products_kernel(places, later, targets, plan, src, adj, *refs):
    slots, block = adj.shape[1] - 1, adj.shape[2]
    rows, slot_bits, target_bits, block_bits = plan_sizes(slots, targets, src.shape[0] // block)
    if later:
        adj_hbm, *outs, tiles, acc, sems = refs
        numbers = [plan[rows + 2, place] for place in later]
        counts = [plan[rows + 1, place] for place in later]
        loads = Tiles(adj_hbm, tiles, sems, numbers, counts)
        loads.start()
    else:
        *outs, acc = refs

    def field(code, start, width):
        return (code >> start) & ((1 << width) - 1)

    def source(number):
        return src[pl.ds(pl.multiple_of(number * block, block), block), :]

    for part, out in enumerate(outs):
        total = out if out.dtype == jnp.float32 else acc
        total[...] = jnp.zeros_like(total)

        @pl.loop(0, (plan[rows, places[part]] + PAIRS - 1) // PAIRS)
        def _(step):
            for lane in range(PAIRS):
                code = plan[step * PAIRS + lane, places[part]]
                half = code >> (slot_bits + block_bits + target_bits)
                one, two = (adj[part, slots - field(c, 0, slot_bits)] for c in (code, half))
                left = jnp.concatenate([one, two], axis=1)
                one, two = (source(field(c, slot_bits, block_bits)) for c in (code, half))
                right = jnp.concatenate([one, two], axis=0)
                start = field(code, slot_bits + block_bits, target_bits) * block
                at = pl.ds(pl.multiple_of(start, block), block)
                total[at, :] += jnp.dot(left, right, preferred_element_type=jnp.float32)

        if total is acc:
            out[...] = acc[...].astype(out.dtype)
    if later:
        loads.wait()


def products(sources, adjacency, tiles, plan, places, later, own):
    block = adjacency.shape[3]
    pieces = len(places)
    feat = sources.shape[1]
    smem, vmem, hbm = (
        pl.BlockSpec(memory_space=space) for space in (pltpu.SMEM, pltpu.VMEM, pltpu.HBM)
    )
    outs = [
        jax.ShapeDtypeStruct((TGT_DEV, feat), jnp.float32 if place < own else jnp.bfloat16)
        for place in places
    ]
    scratch = [pltpu.VMEM((TGT_DEV, feat), jnp.float32)]
    if later:
        outs.append(tiles_shape(adjacency, len(later)))
        scratch.append(tiles_sems(adjacency, len(later)))
    got = pl.pallas_call(
        functools.partial(products_kernel, places, later, TGT_DEV // block),
        in_specs=[smem, vmem, vmem] + ([hbm] if later else []),
        out_specs=[vmem] * len(outs),
        out_shape=outs,
        scratch_shapes=scratch,
        compiler_params=pltpu.CompilerParams(vmem_limit_bytes=PRODUCTS_VMEM),
        cost_estimate=pl.CostEstimate(flops=2**20, bytes_accessed=1024, transcendentals=0),
        name="products",
    )(plan, sources, tiles, *([adjacency] if later else []))
    return list(got[:pieces]), (got[pieces] if later else None)


def pair_sum_kernel(*refs):
    parts = len(refs) // 3
    for own, other, out in zip(refs[:parts], refs[parts : 2 * parts], refs[2 * parts :]):
        out[...] = (own[...] + other[...].astype(jnp.float32)).astype(out.dtype)


def pair_sum(own, others):
    vmem = pl.BlockSpec(memory_space=pltpu.VMEM)
    return pl.pallas_call(
        pair_sum_kernel,
        in_specs=[vmem] * (2 * len(own)),
        out_specs=[vmem] * len(own),
        out_shape=[jax.ShapeDtypeStruct(part.shape, jnp.bfloat16) for part in own],
        compiler_params=pltpu.CompilerParams(vmem_limit_bytes=SMALL_VMEM),
        cost_estimate=pl.CostEstimate(
            flops=own[0].size * len(own), bytes_accessed=6 * own[0].size * len(own), transcendentals=0
        ),
        name="pair_sum",
    )(*own, *others)


def deal_kernel(quarters, first, places, own, *refs):
    others, outs = refs[:-quarters], refs[-quarters:]
    rows = outs[0].shape[0]
    for quarter in range(quarters):
        here = pl.ds(pl.multiple_of(places[first + quarter] * rows, rows), rows)
        total = own[here, :]
        for other in others:
            total += other[here, :].astype(jnp.float32)
        outs[quarter][...] = total.astype(jnp.bfloat16)


def deal(quarters, first, places, own, others):
    rows, feat = own.shape
    vmem = pl.BlockSpec(memory_space=pltpu.VMEM)
    return pl.pallas_call(
        functools.partial(deal_kernel, quarters, first),
        in_specs=[pl.BlockSpec(memory_space=pltpu.SMEM)] + [vmem] * (1 + len(others)),
        out_specs=[vmem] * quarters,
        out_shape=[jax.ShapeDtypeStruct((rows // quarters, feat), jnp.bfloat16)] * quarters,
        compiler_params=pltpu.CompilerParams(vmem_limit_bytes=SMALL_VMEM),
        cost_estimate=pl.CostEstimate(
            flops=own.size * len(others), bytes_accessed=10 * own.size, transcendentals=0
        ),
        name="deal",
    )(places, own, *others)


def layer_kernel(parts, first, places, *refs):
    half = places[first + parts]
    hidden, weights, outs = refs[:parts], refs[parts:-parts - 1], refs[-parts - 1 : -1]
    held = refs[-1]
    depth = hidden[0].shape[1]
    middle = held.shape[1] // 2
    for part, ref in enumerate(hidden):
        at = pl.multiple_of(places[first + part] * depth, depth)
        held[:, pl.ds(at, depth)] = ref[...]
    for part, out in enumerate(outs):
        if part == 0:
            total = jnp.dot(held[...], weights[0][...], preferred_element_type=jnp.float32)
        else:
            total = 0.0
            for side in range(2):
                at = pl.multiple_of((half ^ side) * middle, middle)
                share = weights[2 * part - 1 + side]
                total += jnp.dot(
                    held[:, pl.ds(at, middle)], share[...], preferred_element_type=jnp.float32
                )
        out[...] = jnp.maximum(total, 0.0).astype(out.dtype)


def layer(first, places, hidden, weights):
    parts = len(hidden)
    rows, feat = hidden[0].shape
    depth, columns = weights[0].shape
    vmem = pl.BlockSpec(memory_space=pltpu.VMEM)
    return pl.pallas_call(
        functools.partial(layer_kernel, parts, first),
        in_specs=[pl.BlockSpec(memory_space=pltpu.SMEM)] + [vmem] * (parts + len(weights)),
        out_specs=[vmem] * parts,
        out_shape=[jax.ShapeDtypeStruct((rows, columns), jnp.bfloat16)] * parts,
        scratch_shapes=[pltpu.VMEM((rows, parts * feat), jnp.bfloat16)],
        compiler_params=pltpu.CompilerParams(vmem_limit_bytes=SMALL_VMEM),
        cost_estimate=pl.CostEstimate(
            flops=2 * rows * depth * columns * parts,
            bytes_accessed=2 * parts * depth * columns,
            transcendentals=0,
        ),
        name="layer",
    )(places, *hidden, *weights)


def gather_rows_kernel(first, places, *refs):
    out = refs[-1]
    for part, piece in enumerate(refs[:-1]):
        rows = piece.shape[0]
        out[pl.ds(pl.multiple_of(places[first + part] * rows, rows), rows), :] = piece[...]


def gather_rows(first, places, pieces):
    rows, columns = pieces[0].shape
    vmem = pl.BlockSpec(memory_space=pltpu.VMEM)
    return pl.pallas_call(
        functools.partial(gather_rows_kernel, first),
        in_specs=[pl.BlockSpec(memory_space=pltpu.SMEM)] + [vmem] * len(pieces),
        out_specs=vmem,
        out_shape=jax.ShapeDtypeStruct((rows * len(pieces), columns), pieces[0].dtype),
        compiler_params=pltpu.CompilerParams(vmem_limit_bytes=SMALL_VMEM),
        name="gather_rows",
    )(places, *pieces)


def body(sources, adjacency, target_block, source_block, slot_counts, weight):
    blks, subs, feats = (lax.axis_size(axis) for axis in ("blk", "sub", "feat"))
    blk, sub, feat = (lax.axis_index(axis) for axis in ("blk", "sub", "feat"))
    pieces = [
        forward(blk, part, blks) * subs + forward(sub, step, subs)
        for step in range(subs)
        for part in range(blks)
    ]
    ahead = [forward(feat, step, feats) for step in range(feats)]
    behind = [backward(feat, step, feats) for step in range(feats)]
    places = jnp.stack(pieces + ahead + behind + [sub]).astype(jnp.int32)
    at_ahead, at_behind = len(pieces), len(pieces) + feats

    def exchange(parts, axis):
        size = lax.axis_size(axis)
        got = {step: send(parts[step], axis, step) for step in reversed(range(1, size))}
        return [got[step] for step in range(1, size)]

    far, near = [blks - 1], list(range(blks - 2, 0, -1))
    other = [blks + part for part in range(blks)]
    calls = [
        [other[part] for part in far], far, [other[part] for part in near], near + [other[0]], [0], []
    ]
    plan, held, tiles, share = make_plan(
        target_block, source_block, slot_counts, places, sources, adjacency, weight, subs, calls[0]
    )
    shares = {step: fetch(share, "feat", step) for step in reversed(range(1, feats))}

    def local(number, after):
        nonlocal tiles
        turn, now, *_ = lax.optimization_barrier((plan, tiles, *after))
        made, tiles = products(held, adjacency, now, turn, calls[number], calls[number + 1], blks)
        return made

    others = {}
    away = local(0, [])
    arrived = [send(value, "sub", 1) for value in away]
    kept = local(1, away)
    sums = list(pair_sum(kept, arrived))
    others.update((part, send(value, "blk", part)) for part, value in zip(far, sums))
    away = local(2, sums)
    arrived = [send(value, "sub", 1) for value in away]
    *kept, last = local(3, away)
    sums = list(pair_sum(kept, arrived))
    others.update((part, send(value, "blk", part)) for part, value in zip(near, sums))
    (kept,) = local(4, sums)
    kept, shares = lax.optimization_barrier((kept, shares))
    dealt = deal(feats, at_ahead, places, kept, [send(last, "sub", 1)] + [others[part] for part in range(1, blks)])
    *dealt, shares = lax.optimization_barrier((*dealt, shares))
    hidden = [dealt[0]] + exchange(dealt, "feat")
    weights = [weight]
    for step in range(1, feats):
        weights += [shares[step], send(shares[step], "sub", 1)]
    outs = layer(at_behind, places, hidden, weights)
    done = [outs[0]] + exchange(outs, "feat")
    return gather_rows(at_behind, places, done)


def solution(mesh):
    return jax.shard_map(
        body,
        mesh=mesh,
        in_specs=(
            P(("blk", "sub"), "feat"),
            P(("blk", "sub"), None, None, None, None),
            P(("blk", "sub"), None, None),
            P(("blk", "sub"), None, None),
            P(("blk", "sub"), None),
            P(None, "feat"),
        ),
        out_specs=P(("blk", "sub"), "feat"),
        check_vma=False,
    )
```

time: 321 us -> 83.9 us (0.26)
  matrix products: 108 us -> 0 us
  waiting for transfers between devices: 120 us -> 32.1 us
  local copies, waits for them, and re-layouts: 76 us -> 3.16 us
  Pallas kernels: 0 us -> 28.4 us
  starting transfers between devices: 0.04 us -> 19.1 us
  between operations: 13.4 us -> 0.17 us
    dot_general x4 -> x0, matrix products: 108 us -> none  [the longest x1 55.4 us: one_piece(): jnp.einsum('sij,sjf->sif', adj_piece, selected, preferred_element_type=jn...]
    dot_general x2 -> x0, local copies, waits for them, and re-layouts: 76 us -> none  [the longest x1 66.9 us: one_piece(): jnp.einsum('sij,sjf->sif', adj_piece, selected, preferred_element_type=jn...]
    reduce_scatter x1 -> x0, waiting for transfers between devices: 74.1 us -> none  [body(): lax.psum_scatter(piece_terms.reshape(TGT_DEV * lax.axis_size(('blk', 'sub...]
    all_gather x1 -> x0, waiting for transfers between devices: 46.4 us -> none  [body(): lax.all_gather(hidden, 'feat', axis=1, tiled=True)]
    ppermute x0 -> x19, waiting for transfers between devices: none -> 32.1 us  [the longest x16 27.2 us: send(): lax.ppermute(value, axis, [(i, forward(i, step, size)) for i in range(siz...]
    pallas_call x0 -> x11, Pallas kernels: none -> 28.4 us  [the longest x5 21.2 us: products(): pl.pallas_call(functools.partial(products_kernel, places, later, TGT_DEV...]
    ppermute x0 -> x19, starting transfers between devices: none -> 19.1 us  [the longest x16 11.1 us: send(): lax.ppermute(value, axis, [(i, forward(i, step, size)) for i in range(siz...]
  transfers between devices with their start and end apart: 2 -> 19, of which waited for: 2 -> 7; matrix products, arithmetic and copies ran while one was open for 0% -> 0% of each run, Pallas kernels for 0% -> 16%
where the time goes in v3:
time: 83.9 us; the launch traced here: 83 us
  waiting for transfers between devices  32.1 us (38%)
  Pallas kernels  28.4 us (34%)
  starting transfers between devices  19.1 us (23%)
  local copies, waits for them, and re-layouts  3.16 us (4%)
    ppermute x16, waiting for transfers between devices, send(): lax.ppermute(value, axis, [(i, forward(i, step, size)) for i in range(siz...  27.2 us
    pallas_call x5, Pallas kernels, products(): pl.pallas_call(functools.partial(products_kernel, places, later, TGT_DEV...  21.2 us
    ppermute x16, starting transfers between devices, send(): lax.ppermute(value, axis, [(i, forward(i, step, size)) for i in range(siz...  11.1 us
    ppermute x3, starting transfers between devices, fetch(): lax.ppermute(value, axis, [(forward(i, step, size), i) for i in range(siz...  8.03 us
    ppermute x3, waiting for transfers between devices, fetch(): lax.ppermute(value, axis, [(forward(i, step, size), i) for i in range(siz...  4.97 us
    pallas_call x1, Pallas kernels, make_plan(): pl.pallas_call(functools.partial(plan_kernel, targets, blocks, later), in...  3.36 us
    unnamed x10, local copies, waits for them, and re-layouts  3.07 us
  transfers between devices with their start and end apart: 19, of which 7 were waited for; matrix products, arithmetic and copies ran while one was open for 0% of the time, Pallas kernels for 16%

profile of v3, /device:TPU:0, one launch (start us, length us, event | category | flops | bytes accessed | tf_op | source)
XLA Modules:
  0.0 83.0 jit_solution(3587933130140969441)
XLA Ops:
  0.1 1.0 %copy-done = bf16[1024,256]{1,0:T(8,128)(2,1)S(1)} copy-done((bf16[1024,256]{1,0:T(8,128)(2,1)S(1)}, bf16[1024,256]{1,0:T(8,128)(2,1)}, u32[]{:S(2)}) %copy-start) | copy-done | bytes 524312
  3.2 3.4 %plan.1 = (s32[48,8]{1,0:T(8,128)S(1)}, bf16[8192,256]{1,0:T(8,128)(2,1)S(1)}, bf16[1,65,128,128]{3,2,1,0:T(8,128)(2,1)S(1)}, bf16[512,256]{1,0:T(8,128)(2,1)S(1)}) custom-call(s32[17]{0:T(128)S(1)} %stack.59.ids.places, s32[1,8]{1,0:T(1,128)S(1)} %copy-done.4, s32[1,8,64]{2,1,0:T(8,128)S(1)} %copy-done.2, s32[1,8,64]{2,1,0:T(8,128)S(1)} %copy-done.3, ...), custom_call_target="tpu_custom_call" | custom-call | tf_op jit(solution)/shard_map/plan/pallas_call | solution.py:173
  6.5 3.1 %products.5 = (bf16[1024,256]{1,0:T(8,128)(2,1)S(1)}, bf16[1,65,128,128]{3,2,1,0:T(8,128)(2,1)S(1)}) custom-call(s32[48,8]{1,0:T(8,128)S(1)} %get-tuple-element.74.plan, bf16[8192,256]{1,0:T(8,128)(2,1)S(1)} %get-tuple-element.54.src, bf16[1,65,128,128]{3,2,1,0:T(8,128)(2,1)S(1)} %get-tuple-element.55.adj, bf16[1,8,64,128,128]{4,3,2,1,0:T(8,128)(2,1)} %refs_0_.7), custom_call_target="tpu_custom_call" | custom-call | flops 1048576 | bytes 1024 | tf_op jit(solution)/shard_map/products/pallas_call | solution.py:250
  9.7 3.2 %products.6 = (f32[1024,256]{1,0:T(8,128)S(1)}, bf16[2,65,128,128]{3,2,1,0:T(8,128)(2,1)S(1)}) custom-call(s32[48,8]{1,0:T(8,128)S(1)} %get-tuple-element.74.plan, bf16[8192,256]{1,0:T(8,128)(2,1)S(1)} %get-tuple-element.54.src, bf16[1,65,128,128]{3,2,1,0:T(8,128)(2,1)S(1)} %get-tuple-element.59.adj, bf16[1,8,64,128,128]{4,3,2,1,0:T(8,128)(2,1)} %refs_0_.7), custom_call_target="tpu_custom_call" | custom-call | flops 1048576 | bytes 1024 | tf_op jit(solution)/shard_map/products/pallas_call | solution.py:250
  13.1 5.0 %products.7 = (bf16[1024,256]{1,0:T(8,128)(2,1)S(1)}, bf16[1024,256]{1,0:T(8,128)(2,1)S(1)}, bf16[3,65,128,128]{3,2,1,0:T(8,128)(2,1)S(1)}) custom-call(s32[48,8]{1,0:T(8,128)S(1)} %get-tuple-element.74.plan, bf16[8192,256]{1,0:T(8,128)(2,1)S(1)} %get-tuple-element.54.src, bf16[2,65,128,128]{3,2,1,0:T(8,128)(2,1)S(1)} %get-tuple-element.63.adj, ...), custom_call_target="tpu_custom_call" | custom-call | flops 1048576 | bytes 1024 | tf_op jit(solution)/shard_map/products/pallas_call | solution.py:250
  18.7 3.0 %collective-permute-start.3 = (bf16[512,256]{1,0:T(8,128)(2,1)S(1)}, bf16[512,256]{1,0:T(8,128)(2,1)S(1)}, u32[]{:S(2)}, u32[]{:S(2)}) collective-permute-start(bf16[512,256]{1,0:T(8,128)(2,1)S(1)} %get-tuple-element.76), channel_id=1, source_target_pairs={{1,0},{0,1},{3,2},{2,3},{5,4},{4,5},{7,6},{6,7},{9,8},{8,9},{11,10... | collective-permute-start | bytes 786440 | tf_op jit(solution)/shard_map/ppermute | solution.py:37
  21.7 2.6 %collective-permute-start.4 = (bf16[512,256]{1,0:T(8,128)(2,1)S(1)}, bf16[512,256]{1,0:T(8,128)(2,1)S(1)}, u32[]{:S(2)}, u32[]{:S(2)}) collective-permute-start(bf16[512,256]{1,0:T(8,128)(2,1)S(1)} %get-tuple-element.76), channel_id=1, source_target_pairs={{2,0},{3,1},{0,2},{1,3},{6,4},{7,5},{4,6},{5,7},{10,8},{11,9},{8,1... | collective-permute-start | bytes 786440 | tf_op jit(solution)/shard_map/ppermute | solution.py:37
  24.3 1.9 %collective-permute-start.9 = (bf16[1024,256]{1,0:T(8,128)(2,1)S(1)}, bf16[1024,256]{1,0:T(8,128)(2,1)S(1)}, u32[]{:S(2)}, u32[]{:S(2)}) collective-permute-start(bf16[1024,256]{1,0:T(8,128)(2,1)S(1)} %pair_sum.2), channel_id=1, source_target_pairs={{0,24},{8,16},{16,8},{24,0},{1,25},{9,17},{17,9},{25,1},{2,26},{10... | collective-permute-start | bytes 1572872 | tf_op jit(solution)/shard_map/ppermute | solution.py:32
  26.1 7.4 %products.8 = (f32[1024,256]{1,0:T(8,128)S(1)}, f32[1024,256]{1,0:T(8,128)S(1)}, bf16[1024,256]{1,0:T(8,128)(2,1)S(1)}, bf16[1,65,128,128]{3,2,1,0:T(8,128)(2,1)S(1)}) custom-call(s32[48,8]{1,0:T(8,128)S(1)} %get-tuple-element.74.plan, bf16[8192,256]{1,0:T(8,128)(2,1)S(1)} %get-tuple-element.54.src, bf16[3,65,128,128]{3,2,1,0:T(8,128)(2,1)S(1)} %get-tuple-element.68.adj, ...), custom_call_target="tpu_custom_call" | custom-call | flops 1048576 | bytes 1024 | tf_op jit(solution)/shard_map/products/pallas_call | solution.py:250
  33.9 0.8 collective-permute-start.7
  35.3 1.0 %collective-permute-done.4.refs_7_ = bf16[512,256]{1,0:T(8,128)(2,1)S(1)} collective-permute-done((bf16[512,256]{1,0:T(8,128)(2,1)S(1)}, bf16[512,256]{1,0:T(8,128)(2,1)S(1)}, u32[]{:S(2)}, u32[]{:S(2)}) %collective-permute-start.4) | collective-permute-done | bytes 262176 | tf_op jit(solution)/shard_map/ppermute | solution.py:37
  36.3 2.4 %collective-permute-start.5 = (bf16[512,256]{1,0:T(8,128)(2,1)S(1)}, bf16[512,256]{1,0:T(8,128)(2,1)S(1)}, u32[]{:S(2)}, u32[]{:S(2)}) collective-permute-start(bf16[512,256]{1,0:T(8,128)(2,1)S(1)} %get-tuple-element.76), channel_id=1, source_target_pairs={{3,0},{2,1},{1,2},{0,3},{7,4},{6,5},{5,6},{4,7},{11,8},{10,9},{9,1... | collective-permute-start | bytes 786440 | tf_op jit(solution)/shard_map/ppermute | solution.py:37
  38.7 2.4 %products.9.own = f32[1024,256]{1,0:T(8,128)S(1)} custom-call(s32[48,8]{1,0:T(8,128)S(1)} %get-tuple-element.74.plan, bf16[8192,256]{1,0:T(8,128)(2,1)S(1)} %get-tuple-element.54.src, bf16[1,65,128,128]{3,2,1,0:T(8,128)(2,1)S(1)} %get-tuple-element.75.adj), custom_call_target="tpu_custom_call" | custom-call | flops 1048576 | bytes 1024 | tf_op jit(solution)/shard_map/products/pallas_call | solution.py:250
  41.1 4.0 %collective-permute-done.5.refs_9_ = bf16[512,256]{1,0:T(8,128)(2,1)S(1)} collective-permute-done((bf16[512,256]{1,0:T(8,128)(2,1)S(1)}, bf16[512,256]{1,0:T(8,128)(2,1)S(1)}, u32[]{:S(2)}, u32[]{:S(2)}) %collective-permute-start.5) | collective-permute-done | bytes 262176 | tf_op jit(solution)/shard_map/ppermute | solution.py:37
  45.1 4.9 %collective-permute-done.7.refs_1_ = bf16[1024,256]{1,0:T(8,128)(2,1)S(1)} collective-permute-done((bf16[1024,256]{1,0:T(8,128)(2,1)S(1)}, bf16[1024,256]{1,0:T(8,128)(2,1)S(1)}, u32[]{:S(2)}, u32[]{:S(2)}) %collective-permute-start.7) | collective-permute-done | bytes 524320 | tf_op jit(solution)/shard_map/ppermute | solution.py:32
  50.0 0.8 %deal.1 = (bf16[256,256]{1,0:T(8,128)(2,1)S(1)}, bf16[256,256]{1,0:T(8,128)(2,1)S(1)}, bf16[256,256]{1,0:T(8,128)(2,1)S(1)}, bf16[256,256]{1,0:T(8,128)(2,1)S(1)}) custom-call(s32[17]{0:T(128)S(1)} %stack.59.ids.places, f32[1024,256]{1,0:T(8,128)S(1)} %products.9.own, bf16[1024,256]{1,0:T(8,128)(2,1)S(1)} %collective-permute-done.6.refs_0_, ...), custom_call_target="tpu_custom_call" | custom-call | flops 1048576 | bytes 2621440 | tf_op jit(solution)/shard_map/deal/pallas_call | solution.py:298
  52.3 3.7 %collective-permute-done.10.refs_1_ = bf16[256,256]{1,0:T(8,128)(2,1)S(1)} collective-permute-done((bf16[256,256]{1,0:T(8,128)(2,1)S(1)}, bf16[256,256]{1,0:T(8,128)(2,1)S(1)}, u32[]{:S(2)}, u32[]{:S(2)}) %collective-permute-start.10) | collective-permute-done | bytes 131104 | tf_op jit(solution)/shard_map/ppermute | solution.py:32
  56.2 8.6 %collective-permute-done.11.refs_2_ = bf16[256,256]{1,0:T(8,128)(2,1)S(1)} collective-permute-done((bf16[256,256]{1,0:T(8,128)(2,1)S(1)}, bf16[256,256]{1,0:T(8,128)(2,1)S(1)}, u32[]{:S(2)}, u32[]{:S(2)}) %collective-permute-start.11) | collective-permute-done | bytes 131104 | tf_op jit(solution)/shard_map/ppermute | solution.py:32
  64.8 1.3 %layer.1 = (bf16[256,256]{1,0:T(8,128)(2,1)S(1)}, bf16[256,256]{1,0:T(8,128)(2,1)S(1)}, bf16[256,256]{1,0:T(8,128)(2,1)S(1)}, bf16[256,256]{1,0:T(8,128)(2,1)S(1)}) custom-call(s32[17]{0:T(128)S(1)} %stack.59.ids.places, bf16[256,256]{1,0:T(8,128)(2,1)S(1)} %get-tuple-element.86.refs_0_, bf16[256,256]{1,0:T(8,128)(2,1)S(1)} %collective-permute-done.10.refs_1_, ...), custom_call_target="tpu_custom_call" | custom-call | flops 536870912 | bytes 2097152 | tf_op jit(solution)/shard_map/layer/pallas_call | solution.py:339
  66.1 3.0 %collective-permute-start.16 = (bf16[256,256]{1,0:T(8,128)(2,1)S(1)}, bf16[256,256]{1,0:T(8,128)(2,1)S(1)}, u32[]{:S(2)}, u32[]{:S(2)}) collective-permute-start(bf16[256,256]{1,0:T(8,128)(2,1)S(1)} %get-tuple-element.94), channel_id=1, source_target_pairs={{0,1},{1,0},{2,3},{3,2},{4,5},{5,4},{6,7},{7,6},{8,9},{9,8},{10,11... | collective-permute-start | bytes 393224 | tf_op jit(solution)/shard_map/ppermute | solution.py:32
  69.2 2.4 %collective-permute-start.18 = (bf16[256,256]{1,0:T(8,128)(2,1)S(1)}, bf16[256,256]{1,0:T(8,128)(2,1)S(1)}, u32[]{:S(2)}, u32[]{:S(2)}) collective-permute-start(bf16[256,256]{1,0:T(8,128)(2,1)S(1)} %get-tuple-element.96), channel_id=1, source_target_pairs={{0,3},{1,2},{2,1},{3,0},{4,7},{5,6},{6,5},{7,4},{8,11},{9,10},{10,... | collective-permute-start | bytes 393224 | tf_op jit(solution)/shard_map/ppermute | solution.py:32
  71.6 1.9 %collective-permute-done.16.refs_1_ = bf16[256,256]{1,0:T(8,128)(2,1)S(1)} collective-permute-done((bf16[256,256]{1,0:T(8,128)(2,1)S(1)}, bf16[256,256]{1,0:T(8,128)(2,1)S(1)}, u32[]{:S(2)}, u32[]{:S(2)}) %collective-permute-start.16) | collective-permute-done | bytes 131104 | tf_op jit(solution)/shard_map/ppermute | solution.py:32
  73.5 8.1 %collective-permute-done.17.refs_2_ = bf16[256,256]{1,0:T(8,128)(2,1)S(1)} collective-permute-done((bf16[256,256]{1,0:T(8,128)(2,1)S(1)}, bf16[256,256]{1,0:T(8,128)(2,1)S(1)}, u32[]{:S(2)}, u32[]{:S(2)}) %collective-permute-start.17) | collective-permute-done | bytes 131104 | tf_op jit(solution)/shard_map/ppermute | solution.py:32
  81.6 1.4 %gather_rows.1 = bf16[1024,256]{1,0:T(8,128)(2,1)} custom-call(s32[17]{0:T(128)S(1)} %stack.59.ids.places, bf16[256,256]{1,0:T(8,128)(2,1)S(1)} %get-tuple-element.93.refs_0_, bf16[256,256]{1,0:T(8,128)(2,1)S(1)} %collective-permute-done.16.refs_1_, bf16[256,256]{1,0:T(8,128)(2,1)S(1)} %collective-permute-done.17.refs_2_, ...), custom_call_target="tpu_custom_call" | custom-call | tf_op jit(solution)/shard_map/gather_rows/pallas_call | solution.py:365
  (36 shorter events, 5.4 us)
Async XLA Ops:
  0.1 1.0 %copy-start = (bf16[1024,256]{1,0:T(8,128)(2,1)S(1)}, bf16[1024,256]{1,0:T(8,128)(2,1)}, u32[]{:S(2)}) copy-start(bf16[1024,256]{1,0:T(8,128)(2,1)} %refs_4_.1) | copy-start | bytes 1572868
  1.1 0.7 copy-start.2
  1.8 0.7 copy-start.3
  2.5 0.7 copy-start.4
  9.6 3.3 %collective-permute-start = (bf16[1024,256]{1,0:T(8,128)(2,1)S(1)}, bf16[1024,256]{1,0:T(8,128)(2,1)S(1)}, u32[]{:S(2)}, u32[]{:S(2)}) collective-permute-start(bf16[1024,256]{1,0:T(8,128)(2,1)S(1)} %get-tuple-element.57), channel_id=1, source_target_pairs={{0,4},{4,0},{1,5},{5,1},{2,6},{6,2},{3,7},{7,3},{8,12},{12,8},{9,1... | collective-permute-start | bytes 1572872 | tf_op jit(solution)/shard_map/ppermute | solution.py:32
  18.1 15.5 %collective-permute-start.1 = (bf16[1024,256]{1,0:T(8,128)(2,1)S(1)}, bf16[1024,256]{1,0:T(8,128)(2,1)S(1)}, u32[]{:S(2)}, u32[]{:S(2)}) collective-permute-start(bf16[1024,256]{1,0:T(8,128)(2,1)S(1)} %get-tuple-element.65), channel_id=1, source_target_pairs={{0,4},{4,0},{1,5},{5,1},{2,6},{6,2},{3,7},{7,3},{8,12},{12,8},{9,1... | collective-permute-start | bytes 1572872 | tf_op jit(solution)/shard_map/ppermute | solution.py:32
  18.2 15.5 %collective-permute-start.2 = (bf16[1024,256]{1,0:T(8,128)(2,1)S(1)}, bf16[1024,256]{1,0:T(8,128)(2,1)S(1)}, u32[]{:S(2)}, u32[]{:S(2)}) collective-permute-start(bf16[1024,256]{1,0:T(8,128)(2,1)S(1)} %get-tuple-element.66), channel_id=1, source_target_pairs={{0,4},{4,0},{1,5},{5,1},{2,6},{6,2},{3,7},{7,3},{8,12},{12,8},{9,1... | collective-permute-start | bytes 1572872 | tf_op jit(solution)/shard_map/ppermute | solution.py:32
  18.7 16.0 %collective-permute-start.3 = (bf16[512,256]{1,0:T(8,128)(2,1)S(1)}, bf16[512,256]{1,0:T(8,128)(2,1)S(1)}, u32[]{:S(2)}, u32[]{:S(2)}) collective-permute-start(bf16[512,256]{1,0:T(8,128)(2,1)S(1)} %get-tuple-element.76), channel_id=1, source_target_pairs={{1,0},{0,1},{3,2},{2,3},{5,4},{4,5},{7,6},{6,7},{9,8},{8,9},{11,10... | collective-permute-start | bytes 786440 | tf_op jit(solution)/shard_map/ppermute | solution.py:37
  21.7 14.6 %collective-permute-start.4 = (bf16[512,256]{1,0:T(8,128)(2,1)S(1)}, bf16[512,256]{1,0:T(8,128)(2,1)S(1)}, u32[]{:S(2)}, u32[]{:S(2)}) collective-permute-start(bf16[512,256]{1,0:T(8,128)(2,1)S(1)} %get-tuple-element.76), channel_id=1, source_target_pairs={{2,0},{3,1},{0,2},{1,3},{6,4},{7,5},{4,6},{5,7},{10,8},{11,9},{8,1... | collective-permute-start | bytes 786440 | tf_op jit(solution)/shard_map/ppermute | solution.py:37
  24.3 20.8 %collective-permute-start.9 = (bf16[1024,256]{1,0:T(8,128)(2,1)S(1)}, bf16[1024,256]{1,0:T(8,128)(2,1)S(1)}, u32[]{:S(2)}, u32[]{:S(2)}) collective-permute-start(bf16[1024,256]{1,0:T(8,128)(2,1)S(1)} %pair_sum.2), channel_id=1, source_target_pairs={{0,24},{8,16},{16,8},{24,0},{1,25},{9,17},{17,9},{25,1},{2,26},{10... | collective-permute-start | bytes 1572872 | tf_op jit(solution)/shard_map/ppermute | solution.py:32
  33.6 11.5 %collective-permute-start.6 = (bf16[1024,256]{1,0:T(8,128)(2,1)S(1)}, bf16[1024,256]{1,0:T(8,128)(2,1)S(1)}, u32[]{:S(2)}, u32[]{:S(2)}) collective-permute-start(bf16[1024,256]{1,0:T(8,128)(2,1)S(1)} %get-tuple-element.78), channel_id=1, source_target_pairs={{0,4},{4,0},{1,5},{5,1},{2,6},{6,2},{3,7},{7,3},{8,12},{12,8},{9,1... | collective-permute-start | bytes 1572872 | tf_op jit(solution)/shard_map/ppermute | solution.py:32
  33.9 16.2 %collective-permute-start.7 = (bf16[1024,256]{1,0:T(8,128)(2,1)S(1)}, bf16[1024,256]{1,0:T(8,128)(2,1)S(1)}, u32[]{:S(2)}, u32[]{:S(2)}) collective-permute-start(bf16[1024,256]{1,0:T(8,128)(2,1)S(1)} %get-tuple-element.73), channel_id=1, source_target_pairs={{0,8},{8,0},{16,24},{24,16},{1,9},{9,1},{17,25},{25,17},{2,10},{10... | collective-permute-start | bytes 1572872 | tf_op jit(solution)/shard_map/ppermute | solution.py:32
  34.7 15.4 %collective-permute-start.8 = (bf16[1024,256]{1,0:T(8,128)(2,1)S(1)}, bf16[1024,256]{1,0:T(8,128)(2,1)S(1)}, u32[]{:S(2)}, u32[]{:S(2)}) collective-permute-start(bf16[1024,256]{1,0:T(8,128)(2,1)S(1)} %get-tuple-element.72), channel_id=1, source_target_pairs={{0,16},{8,24},{16,0},{24,8},{1,17},{9,25},{17,1},{25,9},{2,18},{10... | collective-permute-start | bytes 1572872 | tf_op jit(solution)/shard_map/ppermute | solution.py:32
  36.3 8.8 %collective-permute-start.5 = (bf16[512,256]{1,0:T(8,128)(2,1)S(1)}, bf16[512,256]{1,0:T(8,128)(2,1)S(1)}, u32[]{:S(2)}, u32[]{:S(2)}) collective-permute-start(bf16[512,256]{1,0:T(8,128)(2,1)S(1)} %get-tuple-element.76), channel_id=1, source_target_pairs={{3,0},{2,1},{1,2},{0,3},{7,4},{6,5},{5,6},{4,7},{11,8},{10,9},{9,1... | collective-permute-start | bytes 786440 | tf_op jit(solution)/shard_map/ppermute | solution.py:37
  38.7 26.0 %copy-start.1 = (bf16[1024,256]{1,0:T(8,128)(2,1)S(1)}, bf16[1024,256]{1,0:T(8,128)(2,1)}, u32[]{:S(2)}) copy-start(bf16[1024,256]{1,0:T(8,128)(2,1)} %refs_4_.1) | copy-start | bytes 1572868
  50.9 5.1 %collective-permute-start.10 = (bf16[256,256]{1,0:T(8,128)(2,1)S(1)}, bf16[256,256]{1,0:T(8,128)(2,1)S(1)}, u32[]{:S(2)}, u32[]{:S(2)}) collective-permute-start(bf16[256,256]{1,0:T(8,128)(2,1)S(1)} %get-tuple-element.87), channel_id=1, source_target_pairs={{0,1},{1,0},{2,3},{3,2},{4,5},{5,4},{6,7},{7,6},{8,9},{9,8},{10,11... | collective-permute-start | bytes 393224 | tf_op jit(solution)/shard_map/ppermute | solution.py:32
  51.4 13.3 %collective-permute-start.13 = (bf16[512,256]{1,0:T(8,128)(2,1)S(1)}, bf16[512,256]{1,0:T(8,128)(2,1)S(1)}, u32[]{:S(2)}, u32[]{:S(2)}) collective-permute-start(bf16[512,256]{1,0:T(8,128)(2,1)S(1)} %collective-permute-done.3.refs_5_), channel_id=1, source_target_pairs={{0,4},{4,0},{1,5},{5,1},{2,6},{6,2},{3,7},{7,3},{8,12},{12,8},{9,1... | collective-permute-start | bytes 786440 | tf_op jit(solution)/shard_map/ppermute | solution.py:32
  51.4 13.3 %collective-permute-start.14 = (bf16[512,256]{1,0:T(8,128)(2,1)S(1)}, bf16[512,256]{1,0:T(8,128)(2,1)S(1)}, u32[]{:S(2)}, u32[]{:S(2)}) collective-permute-start(bf16[512,256]{1,0:T(8,128)(2,1)S(1)} %collective-permute-done.4.refs_7_), channel_id=1, source_target_pairs={{0,4},{4,0},{1,5},{5,1},{2,6},{6,2},{3,7},{7,3},{8,12},{12,8},{9,1... | collective-permute-start | bytes 786440 | tf_op jit(solution)/shard_map/ppermute | solution.py:32
  51.9 12.8 %collective-permute-start.15 = (bf16[512,256]{1,0:T(8,128)(2,1)S(1)}, bf16[512,256]{1,0:T(8,128)(2,1)S(1)}, u32[]{:S(2)}, u32[]{:S(2)}) collective-permute-start(bf16[512,256]{1,0:T(8,128)(2,1)S(1)} %collective-permute-done.5.refs_9_), channel_id=1, source_target_pairs={{0,4},{4,0},{1,5},{5,1},{2,6},{6,2},{3,7},{7,3},{8,12},{12,8},{9,1... | collective-permute-start | bytes 786440 | tf_op jit(solution)/shard_map/ppermute | solution.py:32
  51.9 12.8 %collective-permute-start.11 = (bf16[256,256]{1,0:T(8,128)(2,1)S(1)}, bf16[256,256]{1,0:T(8,128)(2,1)S(1)}, u32[]{:S(2)}, u32[]{:S(2)}) collective-permute-start(bf16[256,256]{1,0:T(8,128)(2,1)S(1)} %get-tuple-element.88), channel_id=1, source_target_pairs={{0,2},{1,3},{2,0},{3,1},{4,6},{5,7},{6,4},{7,5},{8,10},{9,11},{10,... | collective-permute-start | bytes 393224 | tf_op jit(solution)/shard_map/ppermute | solution.py:32
  55.9 8.8 %collective-permute-start.12 = (bf16[256,256]{1,0:T(8,128)(2,1)S(1)}, bf16[256,256]{1,0:T(8,128)(2,1)S(1)}, u32[]{:S(2)}, u32[]{:S(2)}) collective-permute-start(bf16[256,256]{1,0:T(8,128)(2,1)S(1)} %get-tuple-element.89), channel_id=1, source_target_pairs={{0,3},{1,2},{2,1},{3,0},{4,7},{5,6},{6,5},{7,4},{8,11},{9,10},{10,... | collective-permute-start | bytes 393224 | tf_op jit(solution)/shard_map/ppermute | solution.py:32
  66.1 7.4 %collective-permute-start.16 = (bf16[256,256]{1,0:T(8,128)(2,1)S(1)}, bf16[256,256]{1,0:T(8,128)(2,1)S(1)}, u32[]{:S(2)}, u32[]{:S(2)}) collective-permute-start(bf16[256,256]{1,0:T(8,128)(2,1)S(1)} %get-tuple-element.94), channel_id=1, source_target_pairs={{0,1},{1,0},{2,3},{3,2},{4,5},{5,4},{6,7},{7,6},{8,9},{9,8},{10,11... | collective-permute-start | bytes 393224 | tf_op jit(solution)/shard_map/ppermute | solution.py:32
  69.2 12.4 %collective-permute-start.17 = (bf16[256,256]{1,0:T(8,128)(2,1)S(1)}, bf16[256,256]{1,0:T(8,128)(2,1)S(1)}, u32[]{:S(2)}, u32[]{:S(2)}) collective-permute-start(bf16[256,256]{1,0:T(8,128)(2,1)S(1)} %get-tuple-element.95), channel_id=1, source_target_pairs={{0,2},{1,3},{2,0},{3,1},{4,6},{5,7},{6,4},{7,5},{8,10},{9,11},{10,... | collective-permute-start | bytes 393224 | tf_op jit(solution)/shard_map/ppermute | solution.py:32
  69.2 12.4 %collective-permute-start.18 = (bf16[256,256]{1,0:T(8,128)(2,1)S(1)}, bf16[256,256]{1,0:T(8,128)(2,1)S(1)}, u32[]{:S(2)}, u32[]{:S(2)}) collective-permute-start(bf16[256,256]{1,0:T(8,128)(2,1)S(1)} %get-tuple-element.96), channel_id=1, source_target_pairs={{0,3},{1,2},{2,1},{3,0},{4,7},{5,6},{6,5},{7,4},{8,11},{9,10},{10,... | collective-permute-start | bytes 393224 | tf_op jit(solution)/shard_map/ppermute | solution.py:32
